TPU v7x, 128 devices: a whole 4x4x4 slice. The times are simulated.
128 devices in a mesh: fsdp: 16 (over z, x), ctx: 4 (over y_hi, core), tp: 2 (over y_lo).
Axes of the slice: x: 4, y: 4 (y_hi: 2, y_lo: 2; y = y_hi * 2 + y_lo), z: 4, core: 2. Of those that a mesh axis runs over, the one named last changes fastest.
Arguments:
- tokens: bfloat16 [16384, 2048], P(('fsdp', 'ctx')), may hold values from -6 to 6
- segments: int32 [16384], P(('fsdp', 'ctx')), may hold values from 0 to 2, as said below
- attn_gain: bfloat16 [2048], P('fsdp'), may hold values from 0.5 to 1.5
- q_weight: bfloat16 [2048, 2048], P('fsdp', 'tp'), may hold values from -0.125 to 0.125
- k_weight: bfloat16 [2048, 1024], P('fsdp', 'tp'), may hold values from -0.125 to 0.125
- v_weight: bfloat16 [2048, 1024], P('fsdp', 'tp'), may hold values from -0.125 to 0.125
- q_gain: bfloat16 [128], P('fsdp'), may hold values from 0.099609375 to 1.8984375
- k_gain: bfloat16 [128], P('fsdp'), may hold values from 0.099609375 to 1.8984375
- o_weight: bfloat16 [2048, 2048], P('tp', 'fsdp'), may hold values from -1.5 to 1.5
- mlp_gain: bfloat16 [2048], P('fsdp'), may hold values from 0.5 to 1.5
- gate_weight: bfloat16 [2048, 6144], P('fsdp', 'tp'), may hold values from -0.125 to 0.125
- up_weight: bfloat16 [2048, 6144], P('fsdp', 'tp'), may hold values from -0.125 to 0.125
- down_weight: bfloat16 [6144, 2048], P('tp', 'fsdp'), may hold values from -0.078125 to 0.078125
- cotangent: bfloat16 [16384, 2048], P(('fsdp', 'ctx')), may hold values from -6 to 6
Outputs:
- output: bfloat16 [16384, 2048], P(('fsdp', 'ctx'))
- grad_tokens: float32 [16384, 2048], P(('fsdp', 'ctx'))
- grad_attn_gain: float32 [2048], P('fsdp')
- grad_q_weight: float32 [2048, 2048], P('fsdp', 'tp')
- grad_k_weight: float32 [2048, 1024], P('fsdp', 'tp')
- grad_v_weight: float32 [2048, 1024], P('fsdp', 'tp')
- grad_q_gain: float32 [128], P('fsdp')
- grad_k_gain: float32 [128], P('fsdp')
- grad_o_weight: float32 [2048, 2048], P('tp', 'fsdp')
- grad_mlp_gain: float32 [2048], P('fsdp')
- grad_gate_weight: float32 [2048, 6144], P('fsdp', 'tp')
- grad_up_weight: float32 [2048, 6144], P('fsdp', 'tp')
- grad_down_weight: float32 [6144, 2048], P('tp', 'fsdp')
Inputs may be any that keep to these rules, and one draw needn't show every extreme that they name: `segments`: within each sequence of 1024 tokens the ids are 0, 1, 2 in three unbroken documents in that order; the middle one has 800 tokens and starts at a token from 64 to 160.
All inputs are finite; a program needn't handle non-finite values.
Results may differ from a plain program's by a relative error of at most 0.028.
Values may be sent and summed in bfloat16 or wider, within the bound.
A program may use at most 192 MiB of HBM per device.

v0:
```python
import jax
import jax.numpy as jnp
from jax import lax
from jax.sharding import PartitionSpec as P

QH = 16
KH = 8
HD = 128


epsilon = 1e-06
rope_base = 1000000.0


def scaled_rows(values_in):
    inverse = lax.rsqrt(jnp.mean(values_in * values_in, -1, keepdims=True) + epsilon)
    return (values_in * inverse, inverse)


def norm_back(grad_in, unit_in, inverse):
    return inverse * (grad_in - unit_in * jnp.mean(grad_in * unit_in, -1, keepdims=True))


def rotate(values_in, cosine_table, sine_table, direction):
    half_width = values_in.shape[-1] // 2
    first_half = values_in[..., :half_width]
    second_half = values_in[..., half_width:]
    return jnp.concatenate(
        [
            first_half * cosine_table - direction * second_half * sine_table,
            second_half * cosine_table + direction * first_half * sine_table,
        ],
        -1,
    )


def contract_rows(left_side, right_side):
    return lax.dot_general(
        left_side, right_side, (((0,), (0,)), ((), ())), preferred_element_type=jnp.float32
    )


def contract_cols(left_side, right_side):
    return lax.dot_general(
        left_side, right_side, (((1,), (1,)), ((), ())), preferred_element_type=jnp.float32
    )


def gather_rows(
    attn_gain, q_weight, k_weight, v_weight, q_gain, k_gain, mlp_gain, gate_weight, up_weight
):
    return (
        lax.all_gather(attn_gain, "fsdp", axis=0, tiled=True),
        lax.all_gather(q_weight, "fsdp", axis=0, tiled=True),
        lax.all_gather(k_weight, "fsdp", axis=0, tiled=True),
        lax.all_gather(v_weight, "fsdp", axis=0, tiled=True),
        lax.all_gather(q_gain, "fsdp", axis=0, tiled=True),
        lax.all_gather(k_gain, "fsdp", axis=0, tiled=True),
        lax.all_gather(mlp_gain, "fsdp", axis=0, tiled=True),
        lax.all_gather(gate_weight, "fsdp", axis=0, tiled=True),
        lax.all_gather(up_weight, "fsdp", axis=0, tiled=True),
    )


def gather_cols(o_weight, down_weight):
    return (
        lax.all_gather(o_weight, "fsdp", axis=1, tiled=True),
        lax.all_gather(down_weight, "fsdp", axis=1, tiled=True),
    )


def per_device(
    tokens,
    segments,
    attn_gain,
    q_weight,
    k_weight,
    v_weight,
    q_gain,
    k_gain,
    o_weight,
    mlp_gain,
    gate_weight,
    up_weight,
    down_weight,
    cotangent,
):
    rows_here = tokens.shape[0]
    q_heads = q_weight.shape[1] // HD
    kv_heads = k_weight.shape[1] // HD
    group_size = QH // KH
    score_scale = HD ** (-0.5)
    all_segments = lax.all_gather(segments, "ctx", axis=0, tiled=True)
    seq_len = all_segments.shape[0]
    key_index = jnp.arange(seq_len, dtype=jnp.int32)
    query_index = lax.axis_index("ctx") * rows_here + jnp.arange(rows_here, dtype=jnp.int32)
    earlier = jnp.sum((all_segments[None, :] < segments[:, None]).astype(jnp.int32), axis=1)
    position = query_index - earlier
    frequency = jnp.power(rope_base, -2.0 * jnp.arange(HD // 2, dtype=jnp.float32) / HD)
    angles = position.astype(jnp.float32)[:, None] * frequency[None, :]
    cosine_table = jnp.cos(angles)[:, None, :]
    sine_table = jnp.sin(angles)[:, None, :]
    allowed = (key_index[None, :] <= query_index[:, None]) & (
        all_segments[None, :] == segments[:, None]
    )
    attn_full, wq_full, wk_full, wv_full, qg_full, kg_full, mlp_full, wg_full, wu_full = (
        gather_rows(
            attn_gain,
            q_weight,
            k_weight,
            v_weight,
            q_gain,
            k_gain,
            mlp_gain,
            gate_weight,
            up_weight,
        )
    )
    wo_full, wd_full = gather_cols(o_weight, down_weight)
    hidden_in = tokens.astype(jnp.float32)
    unit_one, inverse_one = scaled_rows(hidden_in)
    normed_one = (unit_one * attn_full.astype(jnp.float32)).astype(jnp.bfloat16)
    query_proj = jnp.dot(normed_one, wq_full, preferred_element_type=jnp.float32).reshape(
        rows_here, q_heads, HD
    )
    key_proj = jnp.dot(normed_one, wk_full, preferred_element_type=jnp.float32).reshape(
        rows_here, kv_heads, HD
    )
    value_rows = jnp.dot(normed_one, wv_full, preferred_element_type=jnp.float32).astype(
        jnp.bfloat16
    )
    query_unit, query_inverse = scaled_rows(query_proj)
    key_unit, key_inverse = scaled_rows(key_proj)
    query_gain_f = qg_full.astype(jnp.float32)
    key_gain_f = kg_full.astype(jnp.float32)
    query_rot = rotate(query_unit * query_gain_f, cosine_table, sine_table, 1.0).astype(
        jnp.bfloat16
    )
    key_rot = (
        rotate(key_unit * key_gain_f, cosine_table, sine_table, 1.0)
        .astype(jnp.bfloat16)
        .reshape(rows_here, kv_heads * HD)
    )
    keys_all, values_all = (
        lax.all_gather(key_rot, "ctx", axis=0, tiled=True),
        lax.all_gather(value_rows, "ctx", axis=0, tiled=True),
    )
    query_four = query_rot.reshape(rows_here, kv_heads, group_size, HD)
    keys_three = keys_all.reshape(seq_len, kv_heads, HD)
    values_three = values_all.reshape(seq_len, kv_heads, HD)
    scores = (
        jnp.einsum("ignd,jgd->gnij", query_four, keys_three, preferred_element_type=jnp.float32)
        * score_scale
    )
    masked = jnp.where(allowed, scores, -jnp.inf)
    row_max = jnp.max(masked, -1, keepdims=True)
    exponent = jnp.exp(masked - row_max)
    row_total = jnp.sum(exponent, -1, keepdims=True)
    probs = exponent / row_total
    log_total = row_max + jnp.log(row_total)
    attended = jnp.einsum(
        "gnij,jgd->ignd",
        probs.astype(jnp.bfloat16),
        values_three,
        preferred_element_type=jnp.float32,
    )
    attended = attended.reshape(rows_here, q_heads * HD).astype(jnp.bfloat16)
    attn_part = jnp.dot(attended, wo_full, preferred_element_type=jnp.float32)
    attn_out = lax.psum(attn_part, "tp")
    middle = hidden_in + attn_out
    unit_two, inverse_two = scaled_rows(middle)
    normed_two = (unit_two * mlp_full.astype(jnp.float32)).astype(jnp.bfloat16)
    gate_act = jnp.dot(normed_two, wg_full, preferred_element_type=jnp.float32)
    up_act = jnp.dot(normed_two, wu_full, preferred_element_type=jnp.float32)
    sigmoid_gate = jax.nn.sigmoid(gate_act)
    silu_gate = gate_act * sigmoid_gate
    product = (silu_gate * up_act).astype(jnp.bfloat16)
    down_part = jnp.dot(product, wd_full, preferred_element_type=jnp.float32)
    mlp_out = lax.psum(down_part.astype(jnp.bfloat16), "tp").astype(jnp.float32)
    result = (middle + mlp_out).astype(jnp.bfloat16)
    grad_out = cotangent.astype(jnp.float32)
    grad_product = contract_cols(cotangent, wd_full)
    grad_down_t = contract_rows(cotangent, product)
    grad_gate = (
        grad_product * up_act * sigmoid_gate * (1.0 + gate_act * (1.0 - sigmoid_gate))
    ).astype(jnp.bfloat16)
    grad_up = (grad_product * silu_gate).astype(jnp.bfloat16)
    grad_two_part = contract_cols(grad_gate, wg_full) + contract_cols(grad_up, wu_full)
    grad_gate_w = contract_rows(normed_two, grad_gate)
    grad_up_w = contract_rows(normed_two, grad_up)
    grad_normed_two = lax.psum(grad_two_part.astype(jnp.bfloat16), "tp").astype(jnp.float32)
    grad_mlp_part = jnp.sum(grad_normed_two * unit_two, 0)
    grad_middle = grad_out + norm_back(
        grad_normed_two * mlp_full.astype(jnp.float32), unit_two, inverse_two
    )
    grad_middle_low = grad_middle.astype(jnp.bfloat16)
    grad_o_t = contract_rows(grad_middle_low, attended)
    grad_attended = contract_cols(grad_middle_low, wo_full).astype(jnp.bfloat16)
    grad_four = grad_attended.reshape(rows_here, kv_heads, group_size, HD)
    scores_again = (
        jnp.einsum("ignd,jgd->gnij", query_four, keys_three, preferred_element_type=jnp.float32)
        * score_scale
    )
    probs_again = jnp.exp(jnp.where(allowed, scores_again - log_total, -jnp.inf))
    probs_low = probs_again.astype(jnp.bfloat16)
    grad_probs = jnp.einsum(
        "ignd,jgd->gnij", grad_four, values_three, preferred_element_type=jnp.float32
    )
    row_dot = jnp.sum(probs_again * grad_probs, -1, keepdims=True)
    grad_scores = (probs_again * (grad_probs - row_dot)).astype(jnp.bfloat16)
    grad_queries = (
        jnp.einsum("gnij,jgd->ignd", grad_scores, keys_three, preferred_element_type=jnp.float32)
        * score_scale
    )
    grad_keys = (
        jnp.einsum("gnij,ignd->jgd", grad_scores, query_four, preferred_element_type=jnp.float32)
        * score_scale
    )
    grad_values = jnp.einsum(
        "gnij,ignd->jgd", probs_low, grad_four, preferred_element_type=jnp.float32
    )
    grad_keys_mine, grad_values_mine = (
        lax.psum_scatter(
            grad_keys.reshape(seq_len, kv_heads * HD).astype(jnp.bfloat16),
            "ctx",
            scatter_dimension=0,
            tiled=True,
        ).astype(jnp.float32),
        lax.psum_scatter(
            grad_values.reshape(seq_len, kv_heads * HD).astype(jnp.bfloat16),
            "ctx",
            scatter_dimension=0,
            tiled=True,
        ).astype(jnp.float32),
    )
    query_back = rotate(
        grad_queries.reshape(rows_here, q_heads, HD), cosine_table, sine_table, -1.0
    )
    grad_qg_part = jnp.sum(query_back * query_unit, (0, 1))
    grad_q_proj = (
        norm_back(query_back * query_gain_f, query_unit, query_inverse)
        .astype(jnp.bfloat16)
        .reshape(rows_here, q_heads * HD)
    )
    key_back = rotate(
        grad_keys_mine.reshape(rows_here, kv_heads, HD), cosine_table, sine_table, -1.0
    )
    grad_kg_part = jnp.sum(key_back * key_unit, (0, 1))
    grad_k_proj = (
        norm_back(key_back * key_gain_f, key_unit, key_inverse)
        .astype(jnp.bfloat16)
        .reshape(rows_here, kv_heads * HD)
    )
    grad_v_proj = grad_values_mine.astype(jnp.bfloat16)
    grad_one_part = (
        contract_cols(grad_q_proj, wq_full)
        + contract_cols(grad_k_proj, wk_full)
        + contract_cols(grad_v_proj, wv_full)
    )
    grad_wq = contract_rows(normed_one, grad_q_proj)
    grad_wk = contract_rows(normed_one, grad_k_proj)
    grad_wv = contract_rows(normed_one, grad_v_proj)
    grad_normed_one, grad_qg_sum, grad_kg_sum = (
        lax.psum(grad_one_part.astype(jnp.bfloat16), "tp").astype(jnp.float32),
        lax.psum(grad_qg_part.astype(jnp.bfloat16), "tp").astype(jnp.float32),
        lax.psum(grad_kg_part.astype(jnp.bfloat16), "tp").astype(jnp.float32),
    )
    grad_attn_part = jnp.sum(grad_normed_one * unit_one, 0)
    grad_input = grad_middle + norm_back(
        grad_normed_one * attn_full.astype(jnp.float32), unit_one, inverse_one
    )
    (
        part_ag,
        part_wq,
        part_wk,
        part_wv,
        part_qg,
        part_kg,
        part_wo,
        part_mg,
        part_wg,
        part_wu,
        part_wd,
    ) = (
        lax.psum_scatter(
            grad_attn_part.astype(jnp.bfloat16), "fsdp", scatter_dimension=0, tiled=True
        ).astype(jnp.float32),
        lax.psum_scatter(
            grad_wq.astype(jnp.bfloat16), "fsdp", scatter_dimension=0, tiled=True
        ).astype(jnp.float32),
        lax.psum_scatter(
            grad_wk.astype(jnp.bfloat16), "fsdp", scatter_dimension=0, tiled=True
        ).astype(jnp.float32),
        lax.psum_scatter(
            grad_wv.astype(jnp.bfloat16), "fsdp", scatter_dimension=0, tiled=True
        ).astype(jnp.float32),
        lax.psum_scatter(
            grad_qg_sum.astype(jnp.bfloat16), "fsdp", scatter_dimension=0, tiled=True
        ).astype(jnp.float32),
        lax.psum_scatter(
            grad_kg_sum.astype(jnp.bfloat16), "fsdp", scatter_dimension=0, tiled=True
        ).astype(jnp.float32),
        lax.psum_scatter(
            grad_o_t.astype(jnp.bfloat16), "fsdp", scatter_dimension=0, tiled=True
        ).astype(jnp.float32),
        lax.psum_scatter(
            grad_mlp_part.astype(jnp.bfloat16), "fsdp", scatter_dimension=0, tiled=True
        ).astype(jnp.float32),
        lax.psum_scatter(
            grad_gate_w.astype(jnp.bfloat16), "fsdp", scatter_dimension=0, tiled=True
        ).astype(jnp.float32),
        lax.psum_scatter(
            grad_up_w.astype(jnp.bfloat16), "fsdp", scatter_dimension=0, tiled=True
        ).astype(jnp.float32),
        lax.psum_scatter(
            grad_down_t.astype(jnp.bfloat16), "fsdp", scatter_dimension=0, tiled=True
        ).astype(jnp.float32),
    )
    sum_ag, sum_wq, sum_wk, sum_wv, sum_qg, sum_kg, sum_wo, sum_mg, sum_wg, sum_wu, sum_wd = (
        lax.psum(part_ag.astype(jnp.bfloat16), "ctx").astype(jnp.float32),
        lax.psum(part_wq.astype(jnp.bfloat16), "ctx").astype(jnp.float32),
        lax.psum(part_wk.astype(jnp.bfloat16), "ctx").astype(jnp.float32),
        lax.psum(part_wv.astype(jnp.bfloat16), "ctx").astype(jnp.float32),
        lax.psum(part_qg.astype(jnp.bfloat16), "ctx").astype(jnp.float32),
        lax.psum(part_kg.astype(jnp.bfloat16), "ctx").astype(jnp.float32),
        lax.psum(part_wo.astype(jnp.bfloat16), "ctx").astype(jnp.float32),
        lax.psum(part_mg.astype(jnp.bfloat16), "ctx").astype(jnp.float32),
        lax.psum(part_wg.astype(jnp.bfloat16), "ctx").astype(jnp.float32),
        lax.psum(part_wu.astype(jnp.bfloat16), "ctx").astype(jnp.float32),
        lax.psum(part_wd.astype(jnp.bfloat16), "ctx").astype(jnp.float32),
    )
    return (
        result,
        grad_input,
        sum_ag,
        sum_wq,
        sum_wk,
        sum_wv,
        sum_qg,
        sum_kg,
        sum_wo.T,
        sum_mg,
        sum_wg,
        sum_wu,
        sum_wd.T,
    )


def solution(mesh):
    placed = (
        P(("fsdp", "ctx"), None),
        P(("fsdp", "ctx")),
        P("fsdp"),
        P("fsdp", "tp"),
        P("fsdp", "tp"),
        P("fsdp", "tp"),
        P("fsdp"),
        P("fsdp"),
        P("tp", "fsdp"),
        P("fsdp"),
        P("fsdp", "tp"),
        P("fsdp", "tp"),
        P("tp", "fsdp"),
        P(("fsdp", "ctx"), None),
    )
    return jax.shard_map(
        per_device,
        mesh=mesh,
        in_specs=placed,
        out_specs=(
            P(("fsdp", "ctx"), None),
            P(("fsdp", "ctx"), None),
            P("fsdp"),
            P("fsdp", "tp"),
            P("fsdp", "tp"),
            P("fsdp", "tp"),
            P("fsdp"),
            P("fsdp"),
            P("tp", "fsdp"),
            P("fsdp"),
            P("fsdp", "tp"),
            P("fsdp", "tp"),
            P("tp", "fsdp"),
        ),
        check_vma=False,
    )
```

profile of v0, /device:TPU:1, one launch (start us, length us, event | category | flops | bytes accessed | tf_op | source)
XLA Modules:
  0.0 1560.2 jit_solution(4273449883446825626)
XLA Ops:
  8.7 18.3 %all-gather = bf16[16,1,128]{2,1,0:T(2,128)(2,1)S(1)} all-gather(bf16[1,1,128]{2,1,0:T(2,128)(2,1)} %bitcast.236), channel_id=1, replica_groups=mesh['fsdp'=16,'ctx'=4,'tp'=2] {'fsdp'}, dimensions={0}, use_global_device_ids=true | all-gather | bytes 4352 | tf_op jit(solution)/shard_map/all_gather | solution.py:53
  28.5 29.1 %all-gather.13.cloned.1.call-done = bf16[2048,512]{1,0:T(8,128)(2,1)} async-done(((bf16[128,512]{1,0:T(8,128)(2,1)}), bf16[2048,512]{1,0:T(8,128)(2,1)}) %all-gather.13.cloned.1.call-update) | async-done | bytes 2097168 | tf_op jit(solution)/shard_map/all_gather | solution.py:56
  57.6 3.5 convolution_convert_fusion.8
  63.5 31.0 %all-reduce.7 = (bf16[128]{0:T(256)(128)(2,1)S(1)}, bf16[128]{0:T(256)(128)(2,1)S(1)}) all-reduce(bf16[128]{0:T(256)(128)(2,1)S(1)} %dynamic-update-slice, bf16[128]{0:T(256)(128)(2,1)S(1)} %dynamic-update-slice.1), channel_id=1, replica_groups=mesh['fsdp'=16,'ctx'=4,'tp'=2] {'fsdp'}, use_global_device_ids=true, to_apply=%add | all-reduce | flops 256 | bytes 1024
  94.5 15.5 all-gather.1
  117.9 10.2 all-gather.15.cloned.1.call-done
  130.2 50.6 %all-gather.21.cloned.1.call-done = bf16[2048,1024]{1,0:T(8,128)(2,1)} async-done(((bf16[128,1024]{1,0:T(8,128)(2,1)}), bf16[2048,1024]{1,0:T(8,128)(2,1)}) %all-gather.21.cloned.1.call-update) | async-done | bytes 4194320 | tf_op jit(solution)/shard_map/all_gather | solution.py:54
  180.8 3.5 fusion.63
  187.0 16.8 %all-gather.19.cloned.1.call-done = bf16[1024,512]{0,1:T(8,128)(2,1)} async-done(((bf16[256,512]{0,1:T(8,128)(2,1)}), bf16[1024,512]{0,1:T(8,128)(2,1)}) %all-gather.19.cloned.1.call-update) | async-done | bytes 1048592 | tf_op jit(solution)/shard_map/all_gather | solution.py:145
  203.8 3.2 fusion.5
  213.1 48.6 %all-gather.23.cloned.1.call-done = bf16[1024,2048]{1,0:T(8,128)(2,1)} async-done(((bf16[1024,128]{1,0:T(8,128)(2,1)}), bf16[1024,2048]{1,0:T(8,128)(2,1)}) %all-gather.23.cloned.1.call-update) | async-done | bytes 4194320 | tf_op jit(solution)/shard_map/all_gather | solution.py:67
  261.6 4.8 fusion.71
  268.5 16.2 %all-gather.2 = bf16[16,1,128]{2,1,0:T(2,128)(2,1)S(1)} all-gather(bf16[1,1,128]{2,1,0:T(2,128)(2,1)S(1)} %bitcast.237), channel_id=1, replica_groups=mesh['fsdp'=16,'ctx'=4,'tp'=2] {'fsdp'}, dimensions={0}, use_global_device_ids=true | all-gather | bytes 4352 | tf_op jit(solution)/shard_map/all_gather | solution.py:59
  284.8 51.5 %all-reduce.17.cloned.1.call-done = f32[256,2048]{1,0:T(8,128)} async-done(((f32[256,2048]{1,0:T(8,128)}), f32[256,2048]{1,0:T(8,128)}) %all-reduce.17.cloned.1.call-update) | async-done | bytes 2097168 | tf_op jit(solution)/shard_map/psum | solution.py:169
  340.0 89.7 %all-gather.25.cloned.1.call-done = bf16[2048,3072]{1,0:T(8,128)(2,1)} async-done(((bf16[128,3072]{1,0:T(8,128)(2,1)}), bf16[2048,3072]{1,0:T(8,128)(2,1)}) %all-gather.25.cloned.1.call-update) | async-done | bytes 12582928 | tf_op jit(solution)/shard_map/all_gather | solution.py:60
  429.7 9.9 fusion.72
  439.7 82.2 %all-gather.27.cloned.1.call-done = bf16[2048,3072]{1,0:T(8,128)(2,1)} async-done(((bf16[128,3072]{1,0:T(8,128)(2,1)}), bf16[2048,3072]{1,0:T(8,128)(2,1)}) %all-gather.27.cloned.1.call-update) | async-done | bytes 12582928 | tf_op jit(solution)/shard_map/all_gather | solution.py:61
  521.8 10.0 fusion.73
  531.8 90.7 %all-gather.29.cloned.1.call-done = bf16[3072,2048]{1,0:T(8,128)(2,1)} async-done(((bf16[3072,128]{1,0:T(8,128)(2,1)}), bf16[3072,2048]{1,0:T(8,128)(2,1)}) %all-gather.29.cloned.1.call-update) | async-done | bytes 12582928 | tf_op jit(solution)/shard_map/all_gather | solution.py:68
  622.6 13.3 multiply_convert_fusion
  635.9 7.4 fusion.74
  643.3 9.0 fusion.20
  653.7 45.6 %all-reduce.19.cloned.1.call-done = bf16[256,2048]{1,0:T(8,128)(2,1)} async-done(((bf16[256,2048]{1,0:T(8,128)(2,1)}), bf16[256,2048]{1,0:T(8,128)(2,1)}) %all-reduce.19.cloned.1.call-update) | async-done | bytes 1048592 | tf_op jit(solution)/shard_map/psum | solution.py:191
  709.1 6.9 bitcast_convert_fusion
  716.3 6.5 fusion
  722.8 5.0 fusion.2
  730.4 9.8 convert_bitcast_fusion
  740.2 16.7 %copy.112 = bf16[2048,3072]{1,0:T(8,128)(2,1)} copy(bf16[2048,3072]{0,1:T(8,128)(2,1)} %convert_bitcast_fusion) | data formatting | bytes 25165824
  757.6 3.2 convolution_convert_fusion.4
  761.1 22.6 %reduce-scatter.12.cloned.1.call-done = bf16[256,512]{0,1:T(8,128)(2,1)} async-done(((bf16[1024,512]{0,1:T(8,128)(2,1)}), bf16[256,512]{0,1:T(8,128)(2,1)}) %reduce-scatter.12.cloned.1.call-update) | async-done | bytes 262160 | tf_op jit(solution)/shard_map/reduce_scatter | solution.py:223
  796.6 3.2 convolution_multiply_fusion
  811.4 3.4 convolution_convert_fusion.3
  814.8 5.1 convolution_convert_fusion.2
  820.2 9.9 convolution_convert_fusion.1
  830.1 10.2 convolution_convert_fusion
  840.4 9.9 convolution_convert_fusion.6
  855.6 25.1 %reduce-scatter.28.cloned.1.call-done = bf16[128,3072]{1,0:T(8,128)(2,1)} async-done(((bf16[2048,3072]{1,0:T(8,128)(2,1)}), bf16[128,3072]{1,0:T(8,128)(2,1)}) %reduce-scatter.28.cloned.1.call-update) | async-done | bytes 786448
  883.1 72.9 %reduce-scatter.20.cloned.1.call-done = bf16[128,512]{1,0:T(8,128)(2,1)} async-done(((bf16[2048,512]{1,0:T(8,128)(2,1)}), bf16[128,512]{1,0:T(8,128)(2,1)}) %reduce-scatter.20.cloned.1.call-update) | async-done | bytes 131088 | tf_op jit(solution)/shard_map/reduce_scatter | solution.py:294
  956.0 77.2 %reduce-scatter.18.cloned.1.call-done = bf16[128,512]{1,0:T(8,128)(2,1)} async-done(((bf16[2048,512]{1,0:T(8,128)(2,1)}), bf16[128,512]{1,0:T(8,128)(2,1)}) %reduce-scatter.18.cloned.1.call-update) | async-done | bytes 131088 | tf_op jit(solution)/shard_map/reduce_scatter | solution.py:291
  1033.1 80.2 %reduce-scatter.16.cloned.1.call-done = bf16[128,1024]{1,0:T(8,128)(2,1)} async-done(((bf16[2048,1024]{1,0:T(8,128)(2,1)}), bf16[128,1024]{1,0:T(8,128)(2,1)}) %reduce-scatter.16.cloned.1.call-update) | async-done | bytes 262160 | tf_op jit(solution)/shard_map/reduce_scatter | solution.py:288
  1113.3 80.6 %reduce-scatter.22.cloned.1.call-done = bf16[128,1024]{1,0:T(8,128)(2,1)} async-done(((bf16[2048,1024]{1,0:T(8,128)(2,1)}), bf16[128,1024]{1,0:T(8,128)(2,1)}) %reduce-scatter.22.cloned.1.call-update) | async-done | bytes 262160 | tf_op jit(solution)/shard_map/reduce_scatter | solution.py:303
  1193.9 98.6 %reduce-scatter.24.cloned.1.call-done = bf16[128,3072]{1,0:T(8,128)(2,1)} async-done(((bf16[2048,3072]{1,0:T(8,128)(2,1)}), bf16[128,3072]{1,0:T(8,128)(2,1)}) %reduce-scatter.24.cloned.1.call-update) | async-done | bytes 786448 | tf_op jit(solution)/shard_map/reduce_scatter | solution.py:309
  1292.6 96.8 %reduce-scatter.26.cloned.1.call-done = bf16[128,3072]{1,0:T(8,128)(2,1)} async-done(((bf16[2048,3072]{1,0:T(8,128)(2,1)}), bf16[128,3072]{1,0:T(8,128)(2,1)}) %reduce-scatter.26.cloned.1.call-update) | async-done | bytes 786448 | tf_op jit(solution)/shard_map/reduce_scatter | solution.py:312
  1390.1 71.9 %all-reduce.23.cloned.1.call-done = (bf16[256,2048]{1,0:T(8,128)(2,1)}, bf16[256,2048]{1,0:T(8,128)(2,1)}) async-done(((bf16[256,2048]{1,0:T(8,128)(2,1)}, bf16[256,2048]{1,0:T(8,128)(2,1)}), (bf16[256,2048]{1,0:T(8,128)(2,1)}, bf16[256,2048]{1,0:T(8,128)(2,1)})) %all-reduce.23.cloned.1.call-update) | async-done | bytes 2097168 | tf_op jit(solution)/shard_map/psum | solution.py:179
  1464.1 34.3 %all-reduce.6 = (bf16[2048]{0:T(1024)(128)(2,1)S(1)}, bf16[128]{0:T(256)(128)(2,1)S(1)}, bf16[128]{0:T(256)(128)(2,1)S(1)}, bf16[2048]{0:T(1024)(128)(2,1)S(1)}) all-reduce(bf16[2048]{0:T(1024)(128)(2,1)S(1)} %get-tuple-element.67, ...), channel_id=4, replica_groups=mesh['fsdp'=16,'ctx'=4,'tp'=2] {'fsdp'}, use_global_device_ids=true, to_apply=%region_19.20.clone | all-reduce | flops 4352 | bytes 17408
  1499.2 4.2 all-reduce.10
  1503.6 15.1 all-reduce.8
  1525.4 19.1 %all-reduce.21.cloned.1.call-done = (bf16[1024,128]{0,1:T(8,128)(2,1)}, bf16[128,1024]{1,0:T(8,128)(2,1)}, bf16[128,512]{1,0:T(8,128)(2,1)}, bf16[128,512]{1,0:T...) async-done(((bf16[1024,128]{0,1:T(8,128)(2,1)}, bf16[128,1024]{1,0:T(8,128)(2,1)}, bf16[128,512]{1,0:T(8,128)(2,1)}, ...) | async-done | bytes 3145744 | tf_op jit(solution)/shard_map/psum | solution.py:326
  (261 shorter events, 93.9 us)
Async XLA Ops:
  7.2 50.4 %all-gather.13.cloned.1.call-start = ((), (), s32[]{:S(2)}) async-start(), calls=%async_computation.9 | async-start | bytes 2228224 | tf_op jit(solution)/shard_map/all_gather | solution.py:56
  7.9 103.5 %all-gather.17.cloned.1.call-start = ((), (), s32[]{:S(2)}) async-start(), calls=%async_computation.11 | async-start | bytes 2228224 | tf_op jit(solution)/shard_map/all_gather | solution.py:55
  8.7 119.4 %all-gather.15.cloned.1.call-start = ((), (), s32[]{:S(2)}) async-start(), calls=%async_computation.10 | async-start | bytes 1310720 | tf_op jit(solution)/shard_map/all_gather | solution.py:146
  28.5 152.3 %copy-start.45 = (f32[256]{0:T(256)}, f32[256]{0:T(256)S(1)}, u32[]{:S(2)}) copy-start(f32[256]{0:T(256)S(1)} %add_rsqrt_fusion.3) | copy-start | bytes 3076
  57.6 4.1 copy-start.56
  57.6 5.4 copy-start.60
  57.6 5.7 copy-start.61
  57.6 36.9 %copy-start.51 = (s32[256]{0:T(256)S(1)}, s32[256]{0:T(256)}, u32[]{:S(2)}) copy-start(s32[256]{0:T(256)} %param.15) | copy-start | bytes 3076
  57.6 53.8 %copy-start.1 = (bf16[256,2048]{1,0:T(8,128)(2,1)S(1)}, bf16[256,2048]{1,0:T(8,128)(2,1)}, u32[]{:S(2)}) copy-start(bf16[256,2048]{1,0:T(8,128)(2,1)} %param.14) | copy-start | bytes 3145732
  61.1 119.7 %all-gather.21.cloned.1.call-start = ((), (), s32[]{:S(2)}) async-start(), calls=%async_computation.13 | async-start | bytes 4456448 | tf_op jit(solution)/shard_map/all_gather | solution.py:54
  61.7 142.1 %all-gather.19.cloned.1.call-start = ((), (), s32[]{:S(2)}) async-start(), calls=%async_computation.12 | async-start | bytes 1310720 | tf_op jit(solution)/shard_map/all_gather | solution.py:145
  94.5 20.1 %copy-start.52 = (f32[128]{0:T(128)}, f32[128]{0:T(128)S(1)}, u32[]{:S(2)}) copy-start(f32[128]{0:T(128)S(1)} %convert_element_type.224) | copy-start | bytes 1540
  111.4 3.6 copy-start.31
  116.8 144.8 %all-gather.23.cloned.1.call-start = ((), (), s32[]{:S(2)}) async-start(), calls=%async_computation.14 | async-start | bytes 4456448 | tf_op jit(solution)/shard_map/all_gather | solution.py:67
  117.3 218.9 %all-reduce.17.cloned.1.call-start = ((), (), s32[]{:S(2)}) async-start(), calls=%async_computation.15 | async-start | bytes 4194304 | tf_op jit(solution)/shard_map/psum | solution.py:169
  117.6 67.7 %copy-start.54 = (f32[128]{0:T(128)}, f32[128]{0:T(128)S(1)}, u32[]{:S(2)}) copy-start(f32[128]{0:T(128)S(1)} %convert_element_type.228) | copy-start | bytes 1540
  186.9 20.1 %copy-start.9 = (bf16[256,8,64]{2,0,1:T(8,128)(2,1)}, bf16[256,8,64]{2,0,1:T(8,128)(2,1)S(1)}, u32[]{:S(2)}) copy-start(bf16[256,8,64]{2,0,1:T(8,128)(2,1)S(1)} %copy.79) | copy-start | bytes 786436
  187.0 20.0 %copy-start.11 = (bf16[256,8,64]{2,0,1:T(8,128)(2,1)}, bf16[256,8,64]{2,0,1:T(8,128)(2,1)S(1)}, u32[]{:S(2)}) copy-start(bf16[256,8,64]{2,0,1:T(8,128)(2,1)S(1)} %copy.78) | copy-start | bytes 786436
  207.0 3.3 copy-start.43
  208.8 4.3 copy-start.47
  213.0 53.3 %copy-start.38 = (bf16[4,128,2,256]{3,1,2,0:T(8,128)(2,1)}, bf16[4,128,2,256]{3,1,2,0:T(8,128)(2,1)S(1)}, u32[]{:S(2)}) copy-start(bf16[4,128,2,256]{3,1,2,0:T(8,128)(2,1)S(1)} %fusion.38) | copy-start | bytes 1572868
  266.4 163.3 %all-gather.25.cloned.1.call-start = ((), (), s32[]{:S(2)}) async-start(), calls=%async_computation.16 | async-start | bytes 13369344 | tf_op jit(solution)/shard_map/all_gather | solution.py:60
  267.2 254.7 %all-gather.27.cloned.1.call-start = ((), (), s32[]{:S(2)}) async-start(), calls=%async_computation.17 | async-start | bytes 13369344 | tf_op jit(solution)/shard_map/all_gather | solution.py:61
  267.9 354.7 %all-gather.29.cloned.1.call-start = ((), (), s32[]{:S(2)}) async-start(), calls=%async_computation.18 | async-start | bytes 13369344 | tf_op jit(solution)/shard_map/all_gather | solution.py:68
  268.5 430.8 %all-reduce.19.cloned.1.call-start = ((), (), s32[]{:S(2)}) async-start(), calls=%async_computation.19 | async-start | bytes 2097152 | tf_op jit(solution)/shard_map/psum | solution.py:191
  635.9 7.4 copy-start.29
  652.3 104.7 %reduce-scatter.14.cloned.1.call-start = ((), (), s32[]{:S(2)}) async-start(), calls=%async_computation.21 | async-start | bytes 1310720 | tf_op jit(solution)/shard_map/reduce_scatter | solution.py:229
  705.0 4.1 copy-start.44
  716.1 67.6 %reduce-scatter.12.cloned.1.call-start = ((), (), s32[]{:S(2)}) async-start(), calls=%async_computation.20 | async-start | bytes 1310720 | tf_op jit(solution)/shard_map/reduce_scatter | solution.py:223
  722.8 5.0 copy-start.10
  722.8 5.0 copy-start.12
  730.4 150.4 %reduce-scatter.28.cloned.1.call-start = ((), (), s32[]{:S(2)}) async-start(), calls=%async_computation.28 | async-start | bytes 13369344
  756.9 4.1 copy-start.53
  757.0 199.0 %reduce-scatter.20.cloned.1.call-start = ((), (), s32[]{:S(2)}) async-start(), calls=%async_computation.24 | async-start | bytes 2228224 | tf_op jit(solution)/shard_map/reduce_scatter | solution.py:294
  760.8 28.6 %copy-start.30 = (f32[256,64]{1,0:T(8,128)S(1)}, f32[256,64]{1,0:T(8,128)}, u32[]{:S(2)}) copy-start(f32[256,64]{1,0:T(8,128)} %get-tuple-element.115) | copy-start | bytes 196612
  760.8 272.3 %reduce-scatter.18.cloned.1.call-start = ((), (), s32[]{:S(2)}) async-start(), calls=%async_computation.23 | async-start | bytes 2228224 | tf_op jit(solution)/shard_map/reduce_scatter | solution.py:291
  785.5 5.5 copy-start.25
  796.5 316.8 %reduce-scatter.16.cloned.1.call-start = ((), (), s32[]{:S(2)}) async-start(), calls=%async_computation.22 | async-start | bytes 4456448 | tf_op jit(solution)/shard_map/reduce_scatter | solution.py:288
  814.8 379.2 %reduce-scatter.22.cloned.1.call-start = ((), (), s32[]{:S(2)}) async-start(), calls=%async_computation.25 | async-start | bytes 4456448 | tf_op jit(solution)/shard_map/reduce_scatter | solution.py:303
  819.9 472.7 %reduce-scatter.24.cloned.1.call-start = ((), (), s32[]{:S(2)}) async-start(), calls=%async_computation.26 | async-start | bytes 13369344 | tf_op jit(solution)/shard_map/reduce_scatter | solution.py:309
  830.1 559.3 %reduce-scatter.26.cloned.1.call-start = ((), (), s32[]{:S(2)}) async-start(), calls=%async_computation.27 | async-start | bytes 13369344 | tf_op jit(solution)/shard_map/reduce_scatter | solution.py:312
  840.4 621.7 %all-reduce.23.cloned.1.call-start = ((), (), s32[]{:S(2)}) async-start(), calls=%async_computation.30 | async-start | bytes 4194304 | tf_op jit(solution)/shard_map/psum | solution.py:179
  840.4 9.9 copy-start.21
  840.4 9.9 copy-start.58
  855.3 689.2 %all-reduce.21.cloned.1.call-start = ((), (), s32[]{:S(2)}) async-start(), calls=%async_computation.29 | async-start | bytes 6291456 | tf_op jit(solution)/shard_map/psum | solution.py:326
  1389.4 74.6 %copy-start.50 = (bf16[2048]{0:T(1024)(128)(2,1)S(1)}, bf16[2048]{0:T(1024)(128)(2,1)}, u32[]{:S(2)}) copy-start(bf16[2048]{0:T(1024)(128)(2,1)} %get-tuple-element.65) | copy-start | bytes 12292
  1544.5 3.9 copy-start.36
  1548.4 3.8 copy-start.41
  (36 other events, 70.2 us)
Sparse Core Ops, SparseCore 0:
  10.2 47.4 all-gather.12
  59.7 44.5 all-gather.16
  106.6 21.4 all-gather.14
  130.1 50.6 all-gather.20
  182.9 20.8 all-gather.18
  205.8 55.8 all-gather.22
  266.5 69.6 all-reduce.16
  338.6 91.1 all-gather.24
  432.1 89.7 all-gather.26
  524.0 98.4 all-gather.28
  652.5 46.7 all-reduce.18
  716.2 32.7 reduce-scatter.13
  752.4 31.2 reduce-scatter.11
  787.0 93.7 reduce-scatter.27
  883.9 72.0 reduce-scatter.19
  959.4 73.6 reduce-scatter.17
  1036.3 76.9 reduce-scatter.15
  1116.9 77.0 reduce-scatter.21
  1197.4 95.1 reduce-scatter.23
  1295.9 93.5 reduce-scatter.25
  1393.1 68.8 all-reduce.22
  1465.9 78.5 all-reduce.20
where the time goes:
time: 1570 us; the launch traced here: 1560 us
  waiting for transfers between devices  1160 us (74%)
  matrix products  148 us (9%)
  blocking collectives  135 us (9%)
  local copies, waits for them, and re-layouts  49.4 us (3%)
  other arithmetic  43.8 us (3%)
  between operations  17.6 us (1%)
    reduce_scatter x1, waiting for transfers between devices, per_device(): lax.psum_scatter(grad_gate_w.astype(jnp.bfloat16), 'fsdp', scatter_dimens...  98.6 us
    reduce_scatter x1, waiting for transfers between devices, per_device(): lax.psum_scatter(grad_up_w.astype(jnp.bfloat16), 'fsdp', scatter_dimensio...  96.8 us
    all_gather x1, waiting for transfers between devices, gather_cols(): lax.all_gather(down_weight, 'fsdp', axis=1, tiled=True)  90.7 us
    all_gather x1, waiting for transfers between devices, gather_rows(): lax.all_gather(gate_weight, 'fsdp', axis=0, tiled=True)  89.7 us
    all_gather x1, waiting for transfers between devices, gather_rows(): lax.all_gather(up_weight, 'fsdp', axis=0, tiled=True)  82.2 us
    reduce_scatter x1, waiting for transfers between devices, per_device(): lax.psum_scatter(grad_o_t.astype(jnp.bfloat16), 'fsdp', scatter_dimension...  80.6 us
    reduce_scatter x1, waiting for transfers between devices, per_device(): lax.psum_scatter(grad_wq.astype(jnp.bfloat16), 'fsdp', scatter_dimension=...  80.2 us
    reduce_scatter x1, waiting for transfers between devices, per_device(): lax.psum_scatter(grad_wk.astype(jnp.bfloat16), 'fsdp', scatter_dimension=...  77.2 us
  transfers between devices with their start and end apart: 22, of which 20 were waited for; matrix products, arithmetic and copies ran while one was open for 11% of the time, Pallas kernels for 0%

commit v1 on v0

v1 whole, which is shorter than its diff:
```python
import jax
import jax.numpy as jnp
from jax import lax
from jax.sharding import PartitionSpec as P

HD = 128
COLUMN = ("ctx", "tp")


epsilon = 1e-06
rope_base = 1000000.0


def scaled_rows(values_in):
    inverse = lax.rsqrt(jnp.mean(values_in * values_in, -1, keepdims=True) + epsilon)
    return (values_in * inverse, inverse)


def norm_back(grad_in, unit_in, inverse):
    return inverse * (grad_in - unit_in * jnp.mean(grad_in * unit_in, -1, keepdims=True))


def rotate(values_in, cosine_table, sine_table, direction):
    half_width = values_in.shape[-1] // 2
    first_half = values_in[..., :half_width]
    second_half = values_in[..., half_width:]
    return jnp.concatenate(
        [
            first_half * cosine_table - direction * second_half * sine_table,
            second_half * cosine_table + direction * first_half * sine_table,
        ],
        -1,
    )


def dot_nn(left, right):
    return jnp.dot(left, right, preferred_element_type=jnp.float32)


def dot_tn(left, right):
    return lax.dot_general(
        left, right, (((0,), (0,)), ((), ())), preferred_element_type=jnp.float32
    )


def dot_nt(left, right):
    return lax.dot_general(
        left, right, (((1,), (1,)), ((), ())), preferred_element_type=jnp.float32
    )


def low(values_in):
    return values_in.astype(jnp.bfloat16)


def full(values_in):
    return values_in.astype(jnp.float32)


def per_device(
    tokens,
    segments,
    attn_gain,
    q_weight,
    k_weight,
    v_weight,
    q_gain,
    k_gain,
    o_weight,
    mlp_gain,
    gate_weight,
    up_weight,
    down_weight,
    cotangent,
):
    part = lax.axis_index("ctx")
    parts = lax.axis_size("ctx")
    half = lax.axis_index("tp")
    halves = lax.axis_size("tp")
    rows_here = tokens.shape[0]
    seq_len = rows_here * parts
    own_rows = rows_here // halves
    score_scale = HD ** (-0.5)

    def quarter(weight, dim):
        size = weight.shape[dim] // parts
        return lax.dynamic_slice_in_dim(weight, part * size, size, dim)

    def own(array):
        return lax.dynamic_slice_in_dim(array, half * own_rows, own_rows, 0)

    attn_gain_f = full(attn_gain)[:, None]
    mlp_gain_f = full(mlp_gain)[:, None]
    wq, wk, wv = quarter(q_weight, 1), quarter(k_weight, 1), quarter(v_weight, 1)
    wg, wu = quarter(gate_weight, 1), quarter(up_weight, 1)
    wo_t = quarter(o_weight, 0).T
    wd_t = quarter(down_weight, 0).T
    w_qkv = jnp.concatenate([wq, wk, wv], 1)
    w_gu = jnp.concatenate([wg, wu], 1)
    send_a = jnp.concatenate([low(full(w_qkv) * attn_gain_f), wo_t], 1)
    send_b = low(full(w_gu) * mlp_gain_f)
    full_a = lax.all_gather(send_a, "fsdp", axis=0, tiled=True)
    full_b = lax.all_gather(send_b, "fsdp", axis=0, tiled=True)
    full_c = lax.all_gather(wd_t, "fsdp", axis=0, tiled=True)
    gains = lax.all_gather(jnp.stack([q_gain, k_gain]), "fsdp", axis=1, tiled=True)
    query_gain_f, key_gain_f = full(gains[0]), full(gains[1])
    nq, nkv, nff = wq.shape[1], wk.shape[1], wg.shape[1]
    full_qkv = full_a[:, : nq + 2 * nkv]
    full_o_t = full_a[:, nq + 2 * nkv :]

    seq_ids = lax.all_gather(segments, "ctx", axis=0, tiled=True)
    index = jnp.arange(seq_len, dtype=jnp.int32)
    count_0 = jnp.sum((seq_ids == 0).astype(jnp.int32))
    count_1 = jnp.sum((seq_ids == 1).astype(jnp.int32))
    position = index - jnp.where(
        seq_ids == 0, 0, jnp.where(seq_ids == 1, count_0, count_0 + count_1)
    )
    frequency = jnp.power(rope_base, -2.0 * jnp.arange(HD // 2, dtype=jnp.float32) / HD)
    angles = position.astype(jnp.float32)[:, None] * frequency[None, :]
    cosine = jnp.cos(angles)[:, None, :]
    sine = jnp.sin(angles)[:, None, :]
    allowed = (index[None, :] <= index[:, None]) & (seq_ids[None, :] == seq_ids[:, None])

    x_here = full(tokens)
    unit_one, inverse_one = scaled_rows(x_here)
    unit_all = lax.all_gather(low(unit_one), "ctx", axis=0, tiled=True)
    grad_out_all = lax.all_gather(cotangent, "ctx", axis=0, tiled=True)
    qkv = dot_nn(unit_all, full_qkv)
    query_proj = qkv[:, :nq].reshape(seq_len, nq // HD, HD)
    key_proj = qkv[:, nq : nq + nkv].reshape(seq_len, nkv // HD, HD)
    values = low(qkv[:, nq + nkv :]).reshape(seq_len, nkv // HD, HD)
    query_unit, query_inverse = scaled_rows(query_proj)
    key_unit, key_inverse = scaled_rows(key_proj)
    group = nq // nkv
    queries = low(rotate(query_unit * query_gain_f, cosine, sine, 1.0))
    keys = low(rotate(key_unit * key_gain_f, cosine, sine, 1.0))
    query_four = queries.reshape(seq_len, nkv // HD, group, HD)
    scores = (
        jnp.einsum("ignd,jgd->gnij", query_four, keys, preferred_element_type=jnp.float32)
        * score_scale
    )
    masked = jnp.where(allowed, scores, -jnp.inf)
    exponent = jnp.exp(masked - jnp.max(masked, -1, keepdims=True))
    probs = exponent / jnp.sum(exponent, -1, keepdims=True)
    attended = low(
        jnp.einsum("gnij,jgd->ignd", low(probs), values, preferred_element_type=jnp.float32)
    ).reshape(seq_len, nq)
    attn_part = low(dot_nt(attended, full_o_t))
    attn_out = lax.psum_scatter(attn_part, COLUMN, scatter_dimension=0, tiled=True)
    middle = own(x_here) + full(attn_out)
    unit_two, inverse_two = scaled_rows(middle)
    two_all = lax.all_gather(low(unit_two), COLUMN, axis=0, tiled=True)
    gate_up = dot_nn(two_all, full_b)
    gate_act, up_act = gate_up[:, :nff], gate_up[:, nff:]
    sigmoid_gate = jax.nn.sigmoid(gate_act)
    silu_gate = gate_act * sigmoid_gate
    product = low(silu_gate * up_act)
    down_part = low(dot_nt(product, full_c))
    mlp_out = lax.psum_scatter(down_part, COLUMN, scatter_dimension=0, tiled=True)
    result = lax.all_gather(low(middle + full(mlp_out)), "tp", axis=0, tiled=True)

    grad_product = dot_nn(grad_out_all, full_c)
    grad_down_t = low(dot_tn(grad_out_all, product))
    grad_gate = low(
        grad_product * up_act * sigmoid_gate * (1.0 + gate_act * (1.0 - sigmoid_gate))
    )
    grad_up = low(grad_product * silu_gate)
    grad_gu = jnp.concatenate([grad_gate, grad_up], 1)
    grad_two_part = low(dot_nt(grad_gu, full_b))
    grad_gu_w = low(dot_tn(two_all, grad_gu))
    grad_two = lax.psum_scatter(grad_two_part, COLUMN, scatter_dimension=0, tiled=True)
    grad_middle = full(own(cotangent)) + norm_back(full(grad_two), unit_two, inverse_two)
    grad_mid_all = lax.all_gather(low(grad_middle), COLUMN, axis=0, tiled=True)
    grad_o_t = low(dot_tn(grad_mid_all, attended))
    grad_attended = low(dot_nn(grad_mid_all, full_o_t))
    grad_four = grad_attended.reshape(seq_len, nkv // HD, group, HD)
    grad_probs = jnp.einsum(
        "ignd,jgd->gnij", grad_four, values, preferred_element_type=jnp.float32
    )
    row_dot = jnp.sum(probs * grad_probs, -1, keepdims=True)
    grad_scores = low(probs * (grad_probs - row_dot))
    grad_queries = (
        jnp.einsum("gnij,jgd->ignd", grad_scores, keys, preferred_element_type=jnp.float32)
        * score_scale
    )
    grad_keys = (
        jnp.einsum("gnij,ignd->jgd", grad_scores, query_four, preferred_element_type=jnp.float32)
        * score_scale
    )
    grad_values = jnp.einsum(
        "gnij,ignd->jgd", low(probs), grad_four, preferred_element_type=jnp.float32
    )
    query_back = rotate(grad_queries.reshape(seq_len, nq // HD, HD), cosine, sine, -1.0)
    grad_qg_part = jnp.sum(query_back * query_unit, (0, 1))
    grad_q_proj = low(norm_back(query_back * query_gain_f, query_unit, query_inverse))
    key_back = rotate(grad_keys, cosine, sine, -1.0)
    grad_kg_part = jnp.sum(key_back * key_unit, (0, 1))
    grad_k_proj = low(norm_back(key_back * key_gain_f, key_unit, key_inverse))
    grad_qkv = jnp.concatenate(
        [
            grad_q_proj.reshape(seq_len, nq),
            grad_k_proj.reshape(seq_len, nkv),
            low(grad_values).reshape(seq_len, nkv),
        ],
        1,
    )
    grad_one_part = low(dot_nt(grad_qkv, full_qkv))
    grad_qkv_w = low(dot_tn(unit_all, grad_qkv))
    grad_one = lax.psum_scatter(grad_one_part, COLUMN, scatter_dimension=0, tiled=True)
    grad_input = grad_middle + norm_back(full(grad_one), own(unit_one), own(inverse_one))
    grad_input = lax.all_gather(grad_input, "tp", axis=0, tiled=True)

    def scatter(grad):
        return lax.psum_scatter(grad, "fsdp", scatter_dimension=0, tiled=True)

    sum_d_t = scatter(grad_down_t)
    sum_gu = scatter(grad_gu_w)
    sum_o_t = scatter(grad_o_t)
    sum_qkv = scatter(grad_qkv_w)
    part_ag = jnp.sum(full(sum_qkv) * full(w_qkv), 1)
    part_mg = jnp.sum(full(sum_gu) * full(w_gu), 1)
    sum_gains = lax.psum(jnp.concatenate([part_ag, part_mg]), COLUMN)
    sum_qk = lax.psum(
        jnp.concatenate([grad_qg_part, grad_kg_part]), ("fsdp", "ctx", "tp")
    ).reshape(2, HD)
    sum_qk = lax.dynamic_slice_in_dim(
        sum_qk, lax.axis_index("fsdp") * q_gain.shape[0], q_gain.shape[0], 1
    )
    own_qkv = low(full(sum_qkv) * attn_gain_f)
    own_gu = low(full(sum_gu) * mlp_gain_f)
    owned = jnp.concatenate([own_qkv, sum_o_t, own_gu, sum_d_t], 1)
    owned = lax.all_gather(owned, "ctx", axis=0, tiled=False)
    rows_w = q_weight.shape[0]

    def columns(start, size):
        piece = owned[:, :, start : start + size]
        return full(jnp.swapaxes(piece, 0, 1).reshape(rows_w, parts * size))

    def rows(start, size):
        piece = owned[:, :, start : start + size]
        return full(jnp.swapaxes(piece, 1, 2).reshape(parts * size, rows_w))

    spots = [0]
    for size in (nq, nkv, nkv, nq, nff, nff, nff):
        spots.append(spots[-1] + size)
    return (
        result,
        grad_input,
        sum_gains[:rows_w],
        columns(spots[0], nq),
        columns(spots[1], nkv),
        columns(spots[2], nkv),
        sum_qk[0],
        sum_qk[1],
        rows(spots[3], nq),
        sum_gains[rows_w:],
        columns(spots[4], nff),
        columns(spots[5], nff),
        rows(spots[6], nff),
    )


def solution(mesh):
    weight = P("fsdp", "tp")
    turned = P("tp", "fsdp")
    acts = P(("fsdp", "ctx"), None)
    gain = P("fsdp")
    return jax.shard_map(
        per_device,
        mesh=mesh,
        in_specs=(
            acts,
            P(("fsdp", "ctx")),
            gain,
            weight,
            weight,
            weight,
            gain,
            gain,
            turned,
            gain,
            weight,
            weight,
            turned,
            acts,
        ),
        out_specs=(
            acts,
            acts,
            gain,
            weight,
            weight,
            weight,
            gain,
            gain,
            turned,
            gain,
            weight,
            weight,
            turned,
        ),
        check_vma=False,
    )
```

time: 1570 us -> 1190 us (0.76)
  waiting for transfers between devices: 1160 us -> 853 us
  matrix products: 148 us -> 107 us
  blocking collectives: 135 us -> 116 us
    psum x4 -> x0, waiting for transfers between devices: 188 us -> none  [the longest x1 71.9 us: per_device(): mlp_out = lax.psum(down_part.astype(jnp.bfloat16), 'tp').astype(jnp.float32)]
    all_gather x9 -> x10, waiting for transfers between devices: 418 us -> 325 us  [the longest x1 71 us: per_device(): two_all = lax.all_gather(low(unit_two), COLUMN, axis=0, tiled=True)]
    psum x2, blocking collectives: 19.4 us -> 86.3 us  [the longest x1 73.3 us: per_device(): lax.psum(jnp.concatenate([grad_qg_part, grad_kg_part]), ('fsdp', 'ctx', '...]
    unnamed x2 -> x0, blocking collectives: 65.3 us -> none
    dot_general x26 -> x17, matrix products: 146 us -> 102 us  [the longest x4 31.4 us: dot_nn(): return jnp.dot(left, right, preferred_element_type=jnp.float32)]
    unnamed x23 -> x18, waiting for transfers between devices: 29.7 us -> 1.48 us
    unnamed x141 -> x150, local copies, waits for them, and re-layouts: 39.8 us -> 13.9 us
    all_gather x3 -> x2, blocking collectives: 49.9 us -> 29.8 us  [the longest x1 18.9 us: per_device(): lax.all_gather(jnp.stack([q_gain, k_gain]), 'fsdp', axis=1, tiled=True)]
  transfers between devices with their start and end apart: 22 -> 18, of which waited for: 20 -> 15; matrix products, arithmetic and copies ran while one was open for 11% -> 11% of each run, Pallas kernels for 0% -> 0%
where the time goes in v1:
time: 1190 us; the launch traced here: 1180 us
  waiting for transfers between devices  853 us (72%)
  blocking collectives  116 us (10%)
  matrix products  107 us (9%)
  other arithmetic  52.5 us (4%)
  local copies, waits for them, and re-layouts  36 us (3%)
  between operations  16.9 us (1%)
    reduce_scatter x4, waiting for transfers between devices, scatter(): return lax.psum_scatter(grad, 'fsdp', scatter_dimension=0, tiled=True)  250 us
    psum x1, blocking collectives, per_device(): lax.psum(jnp.concatenate([grad_qg_part, grad_kg_part]), ('fsdp', 'ctx', '...  73.3 us
    reduce_scatter x1, waiting for transfers between devices, per_device(): lax.psum_scatter(down_part, COLUMN, scatter_dimension=0, tiled=True)  72.2 us
    all_gather x1, waiting for transfers between devices, per_device(): two_all = lax.all_gather(low(unit_two), COLUMN, axis=0, tiled=True)  71 us
    reduce_scatter x1, waiting for transfers between devices, per_device(): lax.psum_scatter(grad_one_part, COLUMN, scatter_dimension=0, tiled=True)  70.7 us
    reduce_scatter x1, waiting for transfers between devices, per_device(): lax.psum_scatter(grad_two_part, COLUMN, scatter_dimension=0, tiled=True)  68.9 us
    reduce_scatter x1, waiting for transfers between devices, per_device(): lax.psum_scatter(attn_part, COLUMN, scatter_dimension=0, tiled=True)  64.8 us
    all_gather x1, waiting for transfers between devices, per_device(): full_b = lax.all_gather(send_b, 'fsdp', axis=0, tiled=True)  61.2 us
  transfers between devices with their start and end apart: 18, of which 15 were waited for; matrix products, arithmetic and copies ran while one was open for 11% of the time, Pallas kernels for 0%

profile of v1, /device:TPU:1, one launch (start us, length us, event | category | flops | bytes accessed | tf_op | source)
XLA Modules:
  0.0 1182.5 jit_solution(17625147286903151259)
XLA Ops:
  14.2 3.2 broadcast_multiply_fusion
  17.5 18.9 %all-gather.2 = bf16[16,8,2]{1,2,0:T(2,128)(2,1)S(1)} all-gather(bf16[1,8,2]{1,2,0:T(2,128)(2,1)S(1)} %maximum_bitcast_fusion.4), channel_id=1, replica_groups=mesh['fsdp'=16,'ctx'=4,'tp'=2] {'fsdp'}, dimensions={0}, use_global_device_ids=true | all-gather | bytes 544 | tf_op jit(solution)/shard_map/all_gather | solution.py:105
  36.5 10.8 all-gather.1
  50.5 3.1 broadcast_multiply_fusion.1
  55.2 8.0 all-gather.16.cloned.1.call-done
  63.2 40.3 %all-gather.14.cloned.1.call-done = bf16[1024,2048]{1,0:T(8,128)(2,1)} async-done(((bf16[256,2048]{1,0:T(8,128)(2,1)}), bf16[1024,2048]{1,0:T(8,128)(2,1)}) %all-gather.14.cloned.1.call-update) | async-done | bytes 4194320 | tf_op jit(solution)/shard_map/all_gather | solution.py:126
  103.5 5.2 fusion.20
  112.2 2.5 copy.97
  123.4 3.0 fusion.23
  127.2 4.5 convolution_convert_fusion.3
  136.0 64.8 %reduce-scatter.9.cloned.1.call-done = bf16[128,2048]{1,0:T(8,128)(2,1)} async-done(((bf16[1024,2048]{1,0:T(8,128)(2,1)}), bf16[128,2048]{1,0:T(8,128)(2,1)}) %reduce-scatter.9.cloned.1.call-update) | async-done | bytes 524304 | tf_op jit(solution)/shard_map/reduce_scatter | solution.py:149
  205.3 61.2 %all-gather.20.cloned.1.call-done = bf16[2048,1536]{1,0:T(8,128)(2,1)} async-done(((bf16[128,1536]{1,0:T(8,128)(2,1)}), bf16[2048,1536]{1,0:T(8,128)(2,1)}) %all-gather.20.cloned.1.call-update) | async-done | bytes 6291472 | tf_op jit(solution)/shard_map/all_gather | solution.py:103
  266.4 71.0 %all-gather.18.cloned.1.call-done = bf16[1024,2048]{1,0:T(8,128)(2,1)} async-done(((bf16[128,2048]{1,0:T(8,128)(2,1)}), bf16[1024,2048]{1,0:T(8,128)(2,1)}) %all-gather.18.cloned.1.call-update) | async-done | bytes 4194320 | tf_op jit(solution)/shard_map/all_gather | solution.py:152
  337.4 11.7 fusion.89
  349.2 44.3 %all-gather.22.cloned.1.call-done = bf16[2048,768]{0,1:T(8,128)(2,1)} async-done(((bf16[128,768]{0,1:T(8,128)(2,1)}), bf16[2048,768]{0,1:T(8,128)(2,1)}) %all-gather.22.cloned.1.call-update) | async-done | bytes 3145744 | tf_op jit(solution)/shard_map/all_gather | solution.py:104
  393.5 40.8 %all-gather.26.cloned.1.call-done = bf16[1024,2048]{1,0:T(8,128)(2,1)} async-done(((bf16[256,2048]{1,0:T(8,128)(2,1)}), bf16[1024,2048]{1,0:T(8,128)(2,1)}) %all-gather.26.cloned.1.call-update) | async-done | bytes 4194320 | tf_op jit(solution)/shard_map/all_gather | solution.py:127
  434.3 10.7 fusion.14
  446.6 8.3 convolution_convert_fusion.1
  455.0 68.9 %reduce-scatter.13.cloned.1.call-done = bf16[128,2048]{1,0:T(8,128)(2,1)} async-done(((bf16[1024,2048]{1,0:T(8,128)(2,1)}), bf16[128,2048]{1,0:T(8,128)(2,1)}) %reduce-scatter.13.cloned.1.call-update) | async-done | bytes 524304 | tf_op jit(solution)/shard_map/reduce_scatter | solution.py:171
  525.3 2.2 fusion.85
  527.5 11.1 convolution_convert_fusion
  539.3 59.3 %all-gather.28.cloned.1.call-done = bf16[1024,2048]{1,0:T(8,128)(2,1)} async-done(((bf16[128,2048]{1,0:T(8,128)(2,1)}), bf16[1024,2048]{1,0:T(8,128)(2,1)}) %all-gather.28.cloned.1.call-update) | async-done | bytes 4194320 | tf_op jit(solution)/shard_map/all_gather | solution.py:173
  598.6 3.8 convolution_convert_fusion.8
  602.5 5.7 fusion
  608.7 2.8 fusion.6
  615.7 2.5 copy.106
  618.3 2.6 fusion.45
  620.9 4.3 fusion.30
  626.8 5.6 fusion.34
  632.4 3.8 convolution_convert_fusion.6
  636.4 7.4 fusion.17
  643.9 4.8 convolution_convert_fusion.7
  648.7 6.0 convolution_convert_fusion.2
  656.2 6.9 convolution_convert_fusion.4
  663.2 20.8 %reduce-scatter.19.cloned.1.call-done = bf16[128,1536]{1,0:T(8,128)(2,1)} async-done(((bf16[2048,1536]{1,0:T(8,128)(2,1)}), bf16[128,1536]{1,0:T(8,128)(2,1)}) %reduce-scatter.19.cloned.1.call-update) | async-done | bytes 393232 | tf_op jit(solution)/shard_map/reduce_scatter | solution.py:214
  685.7 74.8 %reduce-scatter.17.cloned.1.call-done = bf16[128,512]{1,0:T(8,128)(2,1)} async-done(((bf16[2048,512]{1,0:T(8,128)(2,1)}), bf16[128,512]{1,0:T(8,128)(2,1)}) %reduce-scatter.17.cloned.1.call-update) | async-done | bytes 131088 | tf_op jit(solution)/shard_map/reduce_scatter | solution.py:214
  761.6 77.6 %reduce-scatter.23.cloned.1.call-done = bf16[128,768]{1,0:T(8,128)(2,1)} async-done(((bf16[2048,768]{1,0:T(8,128)(2,1)}), bf16[128,768]{1,0:T(8,128)(2,1)}) %reduce-scatter.23.cloned.1.call-update) | async-done | bytes 196624 | tf_op jit(solution)/shard_map/reduce_scatter | solution.py:214
  839.2 76.5 %reduce-scatter.21.cloned.1.call-done = bf16[128,256]{1,0:T(8,128)(2,1)} async-done(((bf16[2048,256]{1,0:T(8,128)(2,1)}), bf16[128,256]{1,0:T(8,128)(2,1)}) %reduce-scatter.21.cloned.1.call-update) | async-done | bytes 65552 | tf_op jit(solution)/shard_map/reduce_scatter | solution.py:214
  918.0 70.7 %reduce-scatter.15.cloned.1.call-done = bf16[128,2048]{1,0:T(8,128)(2,1)} async-done(((bf16[1024,2048]{1,0:T(8,128)(2,1)}), bf16[128,2048]{1,0:T(8,128)(2,1)}) %reduce-scatter.15.cloned.1.call-update) | async-done | bytes 524304 | tf_op jit(solution)/shard_map/reduce_scatter | solution.py:209
  990.2 72.2 %reduce-scatter.11.cloned.1.call-done = bf16[128,2048]{1,0:T(8,128)(2,1)} async-done(((bf16[1024,2048]{1,0:T(8,128)(2,1)}), bf16[128,2048]{1,0:T(8,128)(2,1)}) %reduce-scatter.11.cloned.1.call-update) | async-done | bytes 524304 | tf_op jit(solution)/shard_map/reduce_scatter | solution.py:159
  1062.5 3.0 fusion.42
  1066.2 73.3 %psum.15 = f32[2,128]{1,0:T(2,128)S(1)} all-reduce(f32[2,128]{1,0:T(2,128)S(1)} %maximum_bitcast_fusion.3), channel_id=1, replica_groups=mesh['fsdp'=16,'ctx'=4,'tp'=2] {'fsdp','ctx','tp'}, use_global_device_ids=true, to_apply=%region_27.28 | all-reduce | flops 256 | bytes 2048 | tf_op jit(solution)/shard_map/psum | solution.py:223
  1140.1 13.0 %psum.14 = f32[256]{0:T(256)S(1)} all-reduce(f32[256]{0:T(256)S(1)} %pad_maximum_fusion.15), channel_id=1, replica_groups=mesh['fsdp'=16,'ctx'=4,'tp'=2] {'ctx','tp'}, use_global_device_ids=true, to_apply=%region_21.22 | all-reduce | flops 256 | bytes 2048 | tf_op jit(solution)/shard_map/psum | solution.py:222
  1159.0 3.7 convert_bitcast_fusion
  1162.8 3.0 copy.117
  1165.8 2.7 copy.137
  1169.8 2.3 copy.144
  1172.1 3.1 copy.145
  (252 shorter events, 58.7 us)
Async XLA Ops:
  7.2 196.6 %copy-start = (bf16[3072,128]{1,0:T(8,128)(2,1)S(1)}, bf16[3072,128]{1,0:T(8,128)(2,1)}, u32[]{:S(2)}) copy-start(bf16[3072,128]{1,0:T(8,128)(2,1)} %param.26) | copy-start | bytes 2359300
  7.2 29.3 %copy-start.57 = (s32[256]{0:T(256)S(1)}, s32[256]{0:T(256)}, u32[]{:S(2)}) copy-start(s32[256]{0:T(256)} %param.15) | copy-start | bytes 3076
  7.2 56.0 %all-gather.16.cloned.1.call-start = ((), (), s32[]{:S(2)}) async-start(), calls=%async_computation.9 | async-start | bytes 3342336 | tf_op jit(solution)/shard_map/all_gather | solution.py:102
  8.0 45.6 %copy-start.51 = (f32[128]{0:T(128)}, f32[128]{0:T(128)S(1)}, u32[]{:S(2)}) copy-start(f32[128]{0:T(128)S(1)} %convert_element_type.241) | copy-start | bytes 1540
  8.8 44.7 %copy-start.24 = (bf16[128,256]{1,0:T(8,128)(2,1)}, bf16[128,256]{1,0:T(8,128)(2,1)S(1)}, u32[]{:S(2)}) copy-start(bf16[128,256]{1,0:T(8,128)(2,1)S(1)} %constant_dynamic-slice_fusion.6) | copy-start | bytes 196612
  12.1 91.5 %all-gather.14.cloned.1.call-start = ((), (), s32[]{:S(2)}) async-start(), calls=%async_computation.8 | async-start | bytes 5242880 | tf_op jit(solution)/shard_map/all_gather | solution.py:126
  17.4 183.4 %reduce-scatter.9.cloned.1.call-start = ((), (), s32[]{:S(2)}) async-start(), calls=%async_computation.10 | async-start | bytes 4718592 | tf_op jit(solution)/shard_map/reduce_scatter | solution.py:149
  49.3 54.2 %copy-start.46 = (f32[64]{0:T(128)}, f32[64]{0:T(128)S(1)}, u32[]{:S(2)}) copy-start(f32[64]{0:T(128)S(1)} %multiply_power_fusion) | copy-start | bytes 772
  49.8 60.4 %copy-start.40 = (f32[128]{0:T(128)}, f32[128]{0:T(128)S(1)}, u32[]{:S(2)}) copy-start(f32[128]{0:T(128)S(1)} %get-tuple-element.61) | copy-start | bytes 1540
  108.8 13.3 %copy-start.4 = (f32[1024,512]{0,1:T(8,128)}, f32[1024,512]{0,1:T(8,128)S(1)}, u32[]{:S(2)}) copy-start(f32[1024,512]{0,1:T(8,128)S(1)} %fusion.20) | copy-start | bytes 6291460
  131.7 134.7 %all-gather.20.cloned.1.call-start = ((), (), s32[]{:S(2)}) async-start(), calls=%async_computation.12 | async-start | bytes 6684672 | tf_op jit(solution)/shard_map/all_gather | solution.py:103
  132.4 70.0 %copy-start.54 = (f32[128]{0:T(128)}, f32[128]{0:T(128)S(1)}, u32[]{:S(2)}) copy-start(f32[128]{0:T(128)S(1)} %convert_element_type.258) | copy-start | bytes 1540
  133.4 69.9 %copy-start.18 = (bf16[128,768]{1,0:T(8,128)(2,1)}, bf16[128,768]{1,0:T(8,128)(2,1)S(1)}, u32[]{:S(2)}) copy-start(bf16[128,768]{1,0:T(8,128)(2,1)S(1)} %get-tuple-element.68) | copy-start | bytes 589828
  133.4 69.9 %copy-start.20 = (bf16[128,768]{1,0:T(8,128)(2,1)}, bf16[128,768]{1,0:T(8,128)(2,1)S(1)}, u32[]{:S(2)}) copy-start(bf16[128,768]{1,0:T(8,128)(2,1)S(1)} %get-tuple-element.69) | copy-start | bytes 589828
  134.3 203.1 %all-gather.18.cloned.1.call-start = ((), (), s32[]{:S(2)}) async-start(), calls=%async_computation.11 | async-start | bytes 4718592 | tf_op jit(solution)/shard_map/all_gather | solution.py:152
  202.4 146.8 %copy-start.42 = (f32[128]{0:T(128)}, f32[128]{0:T(128)S(1)}, u32[]{:S(2)}) copy-start(f32[128]{0:T(128)S(1)} %add_rsqrt_fusion.3) | copy-start | bytes 1540
  203.3 190.2 %all-gather.22.cloned.1.call-start = ((), (), s32[]{:S(2)}) async-start(), calls=%async_computation.13 | async-start | bytes 3342336 | tf_op jit(solution)/shard_map/all_gather | solution.py:104
  204.5 229.8 %all-gather.26.cloned.1.call-start = ((), (), s32[]{:S(2)}) async-start(), calls=%async_computation.16 | async-start | bytes 5242880 | tf_op jit(solution)/shard_map/all_gather | solution.py:127
  205.2 318.7 %reduce-scatter.13.cloned.1.call-start = ((), (), s32[]{:S(2)}) async-start(), calls=%async_computation.17 | async-start | bytes 4718592 | tf_op jit(solution)/shard_map/reduce_scatter | solution.py:171
  434.3 12.3 %copy-start.58 = (bf16[2048,1536]{1,0:T(8,128)(2,1)S(1)}, bf16[2048,1536]{1,0:T(8,128)(2,1)}, u32[]{:S(2)}) copy-start(bf16[2048,1536]{1,0:T(8,128)(2,1)} %all-gather.20.cloned.1.call-done) | copy-start | bytes 18874372
  454.9 69.0 %copy-start.43 = (f32[128]{0:T(128)S(1)}, f32[128]{0:T(128)}, u32[]{:S(2)}) copy-start(f32[128]{0:T(128)} %copy-done.42) | copy-start | bytes 1540
  454.9 70.4 %copy-start.11 = (bf16[256,2048]{1,0:T(8,128)(2,1)S(1)}, bf16[256,2048]{1,0:T(8,128)(2,1)}, u32[]{:S(2)}) copy-start(bf16[256,2048]{1,0:T(8,128)(2,1)} %param.27) | copy-start | bytes 3145732
  454.9 143.7 %all-gather.28.cloned.1.call-start = ((), (), s32[]{:S(2)}) async-start(), calls=%async_computation.18 | async-start | bytes 4718592 | tf_op jit(solution)/shard_map/all_gather | solution.py:173
  525.2 13.4 %copy-start.55 = (f32[128]{0:T(128)}, f32[128]{0:T(128)S(1)}, u32[]{:S(2)}) copy-start(f32[128]{0:T(128)S(1)} %broadcast_multiply_fusion.5) | copy-start | bytes 1540
  527.5 156.5 %reduce-scatter.19.cloned.1.call-start = ((), (), s32[]{:S(2)}) async-start(), calls=%async_computation.22 | async-start | bytes 6684672 | tf_op jit(solution)/shard_map/reduce_scatter | solution.py:214
  538.7 221.8 %reduce-scatter.17.cloned.1.call-start = ((), (), s32[]{:S(2)}) async-start(), calls=%async_computation.21 | async-start | bytes 2228224 | tf_op jit(solution)/shard_map/reduce_scatter | solution.py:214
  539.3 63.1 %copy-start.8 = (pred[1024,1024]{0,1:T(8,128)(4,1)S(1)}, pred[1024,1024]{0,1:T(8,128)(4,1)}, u32[]{:S(2)}) copy-start(pred[1024,1024]{0,1:T(8,128)(4,1)} %fusion.11) | copy-start | bytes 3145732
  539.3 63.1 %copy-start.35 = (f32[2,1024]{1,0:T(2,128)S(1)}, f32[2,1024]{1,0:T(2,128)}, u32[]{:S(2)}) copy-start(f32[2,1024]{1,0:T(2,128)} %copy-done.34) | copy-start | bytes 24580
  539.3 63.1 %copy-start.38 = (f32[2,1024]{1,0:T(2,128)S(1)}, f32[2,1024]{1,0:T(2,128)}, u32[]{:S(2)}) copy-start(f32[2,1024]{1,0:T(2,128)} %copy-done.37) | copy-start | bytes 24580
  636.3 202.9 %reduce-scatter.23.cloned.1.call-start = ((), (), s32[]{:S(2)}) async-start(), calls=%async_computation.24 | async-start | bytes 3342336 | tf_op jit(solution)/shard_map/reduce_scatter | solution.py:214
  643.8 271.8 %reduce-scatter.21.cloned.1.call-start = ((), (), s32[]{:S(2)}) async-start(), calls=%async_computation.23 | async-start | bytes 1114112 | tf_op jit(solution)/shard_map/reduce_scatter | solution.py:214
  648.7 340.0 %reduce-scatter.15.cloned.1.call-start = ((), (), s32[]{:S(2)}) async-start(), calls=%async_computation.19 | async-start | bytes 4718592 | tf_op jit(solution)/shard_map/reduce_scatter | solution.py:209
  654.8 407.7 %reduce-scatter.11.cloned.1.call-start = ((), (), s32[]{:S(2)}) async-start(), calls=%async_computation.14 | async-start | bytes 4718592 | tf_op jit(solution)/shard_map/reduce_scatter | solution.py:159
  663.1 20.9 %copy-start.19 = (bf16[128,768]{1,0:T(8,128)(2,1)S(1)}, bf16[128,768]{1,0:T(8,128)(2,1)}, u32[]{:S(2)}) copy-start(bf16[128,768]{1,0:T(8,128)(2,1)} %copy-done.18) | copy-start | bytes 589828
  663.1 20.9 %copy-start.21 = (bf16[128,768]{1,0:T(8,128)(2,1)S(1)}, bf16[128,768]{1,0:T(8,128)(2,1)}, u32[]{:S(2)}) copy-start(bf16[128,768]{1,0:T(8,128)(2,1)} %copy-done.20) | copy-start | bytes 589828
  663.1 97.5 %copy-start.25 = (bf16[128,256]{1,0:T(8,128)(2,1)S(1)}, bf16[128,256]{1,0:T(8,128)(2,1)}, u32[]{:S(2)}) copy-start(bf16[128,256]{1,0:T(8,128)(2,1)} %copy-done.24) | copy-start | bytes 196612
  663.1 97.5 %copy-start.31 = (bf16[128,128]{1,0:T(8,128)(2,1)S(1)}, bf16[128,128]{1,0:T(8,128)(2,1)}, u32[]{:S(2)}) copy-start(bf16[128,128]{1,0:T(8,128)(2,1)} %copy-done.30) | copy-start | bytes 98308
  663.1 97.5 %copy-start.33 = (bf16[128,128]{1,0:T(8,128)(2,1)S(1)}, bf16[128,128]{1,0:T(8,128)(2,1)}, u32[]{:S(2)}) copy-start(bf16[128,128]{1,0:T(8,128)(2,1)} %copy-done.32) | copy-start | bytes 98308
  663.1 97.5 %copy-start.52 = (f32[128]{0:T(128)S(1)}, f32[128]{0:T(128)}, u32[]{:S(2)}) copy-start(f32[128]{0:T(128)} %copy-done.51) | copy-start | bytes 1540
  663.1 254.8 %copy-start.50 = (f32[256]{0:T(256)S(1)}, f32[256]{0:T(256)}, u32[]{:S(2)}) copy-start(f32[256]{0:T(256)} %copy-done.49) | copy-start | bytes 3076
  663.1 399.4 %copy-start.10 = (bf16[128,2048]{1,0:T(8,128)(2,1)S(1)}, bf16[128,2048]{1,0:T(8,128)(2,1)}, u32[]{:S(2)}) copy-start(bf16[128,2048]{1,0:T(8,128)(2,1)} %reduce-scatter.13.cloned.1.call-done) | copy-start | bytes 1572868
  663.1 399.4 %copy-start.12 = (bf16[256,2048]{1,0:T(8,128)(2,1)S(1)}, bf16[256,2048]{1,0:T(8,128)(2,1)}, u32[]{:S(2)}) copy-start(bf16[256,2048]{1,0:T(8,128)(2,1)} %param.27) | copy-start | bytes 3145732
  663.1 399.3 %copy-start.44 = (f32[128]{0:T(128)S(1)}, f32[128]{0:T(128)}, u32[]{:S(2)}) copy-start(f32[128]{0:T(128)} %copy-done.42) | copy-start | bytes 1540
  663.2 490.4 %all-gather.32.cloned.1.call-start = ((), (), s32[]{:S(2)}) async-start(), calls=%async_computation.25 | async-start | bytes 3932160 | tf_op jit(solution)/shard_map/all_gather | solution.py:232
  917.6 252.2 %all-gather.24.cloned.1.call-start = ((), (), s32[]{:S(2)}) async-start(), calls=%async_computation.15 | async-start | bytes 1572864 | tf_op jit(solution)/shard_map/all_gather | solution.py:160
  988.6 77.5 %copy-start.56 = (f32[256]{0:T(256)S(1)}, f32[256]{0:T(256)}, u32[]{:S(2)}) copy-start(f32[256]{0:T(256)} %get-tuple-element.26) | copy-start | bytes 3076
  988.6 151.4 %copy-start.53 = (f32[128]{0:T(128)S(1)}, f32[128]{0:T(128)}, u32[]{:S(2)}) copy-start(f32[128]{0:T(128)} %get-tuple-element.48) | copy-start | bytes 1540
  1065.5 104.3 %all-gather.30.cloned.1.call-start = ((), (), s32[]{:S(2)}) async-start(), calls=%async_computation.20 | async-start | bytes 3145728 | tf_op jit(solution)/shard_map/all_gather | solution.py:211
  (43 other events, 184.4 us)
Sparse Core Ops, SparseCore 0:
  12.2 50.9 all-gather.15
  65.4 38.0 all-gather.13
  131.9 68.8 reduce-scatter.8
  203.3 63.0 all-gather.19
  268.5 68.9 all-gather.17
  340.0 53.4 all-gather.21
  395.2 39.0 all-gather.25
  455.0 68.8 reduce-scatter.12
  527.6 71.0 all-gather.27
  601.9 82.0 reduce-scatter.18
  687.3 73.2 reduce-scatter.16
  764.1 75.0 reduce-scatter.22
  843.3 72.3 reduce-scatter.20
  917.9 70.6 reduce-scatter.14
  990.9 71.5 reduce-scatter.10
  1064.6 35.2 all-gather.31
  1101.3 22.7 all-gather.23
  1126.2 36.9 all-gather.29

commit v2 on v1

v2 whole, which is shorter than its diff:
```python
import functools

import jax
import jax.numpy as jnp
from jax import lax
from jax.experimental import pallas as pl
from jax.experimental.pallas import tpu as pltpu
from jax.sharding import PartitionSpec as P

HD = 128
MESH = pl.DeviceIdType.MESH
HBM = pl.BlockSpec(memory_space=pl.ANY)
VMEM = pl.BlockSpec(memory_space=pltpu.VMEM)
LOW = jnp.bfloat16
WIDE = jnp.float32


epsilon = 1e-06
rope_base = 1000000.0


def scaled_rows(values_in):
    inverse = lax.rsqrt(jnp.mean(values_in * values_in, -1, keepdims=True) + epsilon)
    return (values_in * inverse, inverse)


def norm_back(grad_in, unit_in, inverse):
    return inverse * (grad_in - unit_in * jnp.mean(grad_in * unit_in, -1, keepdims=True))


def rotate(values_in, cosine_table, sine_table, direction):
    half_width = values_in.shape[-1] // 2
    first_half = values_in[..., :half_width]
    second_half = values_in[..., half_width:]
    return jnp.concatenate(
        [
            first_half * cosine_table - direction * second_half * sine_table,
            second_half * cosine_table + direction * first_half * sine_table,
        ],
        -1,
    )


def dot_nn(left, right):
    return jnp.dot(left, right, preferred_element_type=WIDE)


def dot_tn(left, right):
    return lax.dot_general(left, right, (((0,), (0,)), ((), ())), preferred_element_type=WIDE)


def dot_nt(left, right):
    return lax.dot_general(left, right, (((1,), (1,)), ((), ())), preferred_element_type=WIDE)


def low(values_in):
    return values_in.astype(LOW)


def full(values_in):
    return values_in.astype(WIDE)


def place():
    plane = lax.axis_index("fsdp")
    part = lax.axis_index("ctx")
    half = lax.axis_index("tp")
    return {
        "z": lax.div(plane, 4),
        "x": lax.rem(plane, 4),
        "y": lax.div(part, 2) * 2 + half,
        "core": lax.rem(part, 2),
    }


def device(where):
    return (
        where["z"] * 4 + where["x"],
        lax.div(where["y"], 2) * 2 + where["core"],
        lax.rem(where["y"], 2),
    )


def moved(here, axis, step):
    there = dict(here)
    if axis == "pair":
        there["y"] = here["y"] + 1 - 2 * lax.rem(here["y"], 2)
    elif axis == "core":
        there["core"] = 1 - here["core"]
    else:
        there[axis] = lax.rem(here[axis] + step, 4)
    return there


def block_of(y, core):
    return lax.div(y, 2) * 4 + core * 2 + lax.rem(y, 2)


class Links:
    def __init__(self, send_sems, recv_sems):
        self.here = place()
        self.send_sems, self.recv_sems = send_sems, recv_sems
        self.started = []

    def meet(self, peers):
        barrier = pltpu.get_barrier_semaphore()
        for axis, step in peers:
            pl.semaphore_signal(
                barrier,
                inc=1,
                device_id=device(moved(self.here, axis, step)),
                device_id_type=MESH,
            )
        pl.semaphore_wait(barrier, len(peers))

    def send(self, src, dst, axis, step=0):
        spot = len(self.started)
        copy = pltpu.make_async_remote_copy(
            src_ref=src,
            dst_ref=dst,
            send_sem=self.send_sems.at[spot],
            recv_sem=self.recv_sems.at[spot],
            device_id=device(moved(self.here, axis, step)),
            device_id_type=MESH,
        )
        copy.start()
        self.started.append(copy)
        return copy

    def drain(self):
        for copy in self.started:
            copy.wait_send()


PLANE = [("x", 1), ("x", 2), ("x", 3), ("z", 1), ("z", 2), ("z", 3)]
COLUMN = [("y", 1), ("y", 2), ("y", 3), ("core", 0)]


def together(jobs):
    jobs = list(jobs)
    while jobs:
        left = []
        for job in jobs:
            try:
                next(job)
                left.append(job)
            except StopIteration:
                pass
        jobs = left


def each(count, step, body):
    def one(i, carry):
        body(pl.ds(pl.multiple_of(i * step, step), step))
        return carry

    lax.fori_loop(0, count // step, one, 0)


def add_rows(into, first, second):
    lead, rows = into.shape[:-2], into.shape[-2]

    def add(spot):
        def body(window):
            spots = spot + (window,)
            into[spots] = low(full(first[spots]) + full(second[spots]))

        return body

    if not lead:
        each(rows, 16, add(()))
    else:
        for i in range(lead[0]):
            each(rows, 16, add((i,)))


def gather4(links, axis, own, block, arrived=None):
    me = links.here[axis]
    before, after, far = lax.rem(me + 3, 4), lax.rem(me + 1, 4), lax.rem(me + 2, 4)
    arrived = arrived or (lambda spot, side: None)
    up, down = {}, {}
    up[0] = links.send(own(0), block(me, 0), axis, 1)
    down[1] = links.send(own(1), block(me, 1), axis, 3)
    up[1] = links.send(own(1), block(me, 1), axis, 1)
    down[0] = links.send(own(0), block(me, 0), axis, 3)
    yield
    up[0].wait_recv()
    up_far = links.send(block(before, 0), block(before, 0), axis, 1)
    arrived(before, 0)
    down[1].wait_recv()
    down_far = links.send(block(after, 1), block(after, 1), axis, 3)
    arrived(after, 1)
    yield
    up[1].wait_recv()
    arrived(before, 1)
    down[0].wait_recv()
    arrived(after, 0)
    yield
    up_far.wait_recv()
    arrived(far, 0)
    down_far.wait_recv()
    arrived(far, 1)


def scatter4(links, axis, mine, near, far):
    me = links.here[axis]
    before, after, beyond = lax.rem(me + 3, 4), lax.rem(me + 1, 4), lax.rem(me + 2, 4)
    up_far = links.send(mine(beyond, 0), far[0], axis, 1)
    down_far = links.send(mine(beyond, 1), far[1], axis, 3)
    up_one = links.send(mine(after, 1), near[0](1), axis, 1)
    down_one = links.send(mine(before, 0), near[1](0), axis, 3)
    yield
    up_far.wait_recv()
    add_rows(far[0], far[0], mine(after, 0))
    up_two = links.send(far[0], near[0](0), axis, 1)
    down_far.wait_recv()
    add_rows(far[1], far[1], mine(before, 1))
    down_two = links.send(far[1], near[1](1), axis, 3)
    yield
    up_one.wait_recv()
    down_one.wait_recv()
    yield
    up_two.wait_recv()
    down_two.wait_recv()


def column_gather(links, own_ref, out):
    here = links.here
    rows = out.shape[1] // 2
    shared = []

    def own(h):
        return own_ref.at[pl.ds(h * rows, rows)]

    def block(p, h):
        return out.at[block_of(p, here["core"]), pl.ds(h * rows, rows)]

    def arrived(p, h):
        shared.append(links.send(block(p, h), block(p, h), "core"))

    ring = gather4(links, "y", own, block, arrived)
    next(ring)
    for h in range(2):
        shared.append(links.send(own(h), block(here["y"], h), "core"))
    yield
    for _ in ring:
        yield
    yield
    for copy in shared:
        copy.wait_recv()


def column_scatter(links, partial, passed, near, far, done):
    here = links.here
    rows = partial.shape[1] // 2
    core = here["core"]
    me = here["y"]
    order = [lax.rem(me + step, 4) for step in (2, 1, 3, 0)]
    over = [
        links.send(partial.at[block_of(p, 1 - core)], passed.at[p], "core") for p in order
    ]
    yield
    for copy, p in zip(over[:3], order[:3]):
        copy.wait_recv()
        add_rows(passed.at[p], passed.at[p], partial.at[block_of(p, core)])
    ring = scatter4(
        links,
        "y",
        lambda p, h: passed.at[p, pl.ds(h * rows, rows)],
        [lambda h, i=i: near.at[i, pl.ds(h * rows, rows)] for i in range(2)],
        [far.at[0], far.at[1]],
    )
    for _ in ring:
        yield
    over[3].wait_recv()
    own = partial.at[block_of(me, core)]
    mine = passed.at[me]

    def body(window):
        done(
            window,
            (full(own[window]) + full(mine[window]))
            + (full(near[0, window]) + full(near[1, window])),
        )

    each(2 * rows, 16, body)


def plane_gather(links, own_ref, out, local_sem):
    here = links.here
    z, x = here["z"], here["x"]
    width = own_ref.shape[1] // 2
    rows = own_ref.shape[0] // 2
    kept = pltpu.make_async_copy(own_ref, out.at[z, x], local_sem)
    kept.start()
    sides = [pl.ds(0, width), pl.ds(width, width)]

    def own(side):
        return lambda h: own_ref.at[pl.ds(h * rows, rows), side]

    first = [
        gather4(
            links, "x", own(sides[0]), lambda p, h: out.at[z, p, pl.ds(h * rows, rows), sides[0]]
        ),
        gather4(
            links, "z", own(sides[1]), lambda p, h: out.at[p, x, pl.ds(h * rows, rows), sides[1]]
        ),
    ]
    for _ in zip(*first):
        yield
    together(first)
    kept.wait()

    def by_z(p, h):
        return out.at[p, pl.ds(2 * h, 2), :, sides[0]]

    def by_x(p, h):
        return out.at[pl.ds(2 * h, 2), p, :, sides[1]]

    second = [
        gather4(links, "z", lambda h: by_z(z, h), by_z),
        gather4(links, "x", lambda h: by_x(x, h), by_x),
    ]
    for _ in zip(*second):
        yield
    together(second)


def plane_scratch(width):
    half = width // 2
    return [
        pltpu.VMEM((2, 2, 4, 128, half), LOW),
        pltpu.VMEM((2, 2, 2, 128, half), LOW),
        pltpu.VMEM((2, 4, 128, half), LOW),
        pltpu.VMEM((2, 2, 128, half), LOW),
        pltpu.VMEM((2, 2, 64, half), LOW),
    ]


def plane_scatter(links, grad, out, near, far, middle, near_two, far_two):
    here = links.here
    z, x = here["z"], here["x"]
    half = out.shape[1] // 2
    sides = [pl.ds(0, half), pl.ds(half, half)]
    first = [
        scatter4(
            links,
            "x",
            lambda p, h: grad.at[pl.ds(2 * h, 2), p, :, sides[0]],
            [lambda h, i=i: near.at[0, i, pl.ds(2 * h, 2)] for i in range(2)],
            [far.at[0, 0], far.at[0, 1]],
        ),
        scatter4(
            links,
            "z",
            lambda p, h: grad.at[p, pl.ds(2 * h, 2), :, sides[1]],
            [lambda h, i=i: near.at[1, i, pl.ds(2 * h, 2)] for i in range(2)],
            [far.at[1, 0], far.at[1, 1]],
        ),
    ]
    for _ in zip(*first):
        yield
    together(first)
    for s in range(2):
        for p in range(4):
            own = grad.at[p, x, :, sides[0]] if s == 0 else grad.at[z, p, :, sides[1]]

            def body(window, s=s, p=p, own=own):
                middle[s, p, window] = low(
                    full(own[window])
                    + (full(near[s, 0, p, window]) + full(near[s, 1, p, window]))
                )

            each(128, 16, body)
    second = [
        scatter4(
            links,
            axis,
            lambda p, h, s=s: middle.at[s, p, pl.ds(h * 64, 64)],
            [lambda h, s=s, i=i: near_two.at[s, i, pl.ds(h * 64, 64)] for i in range(2)],
            [far_two.at[s, 0], far_two.at[s, 1]],
        )
        for s, axis in enumerate(("z", "x"))
    ]
    for _ in zip(*second):
        yield
    together(second)
    for s, me in enumerate((z, x)):

        def body(window, s=s, me=me):
            out[window, sides[s]] = low(
                full(middle[s, me, window])
                + (full(near_two[s, 0, window]) + full(near_two[s, 1, window]))
            )

        each(128, 16, body)


def column_scratch():
    return [
        pltpu.VMEM((4, 128, 2048), LOW),
        pltpu.VMEM((2, 128, 2048), LOW),
        pltpu.VMEM((2, 64, 2048), LOW),
    ]


def small_plane(links, own, out):
    z, x = links.here["z"], links.here["x"]
    out[z, x] = own[...]
    copies = [links.send(own, out.at[z, x], "x", step) for step in (1, 2, 3)]
    yield
    for copy in copies:
        copy.wait_recv()
    copies = [links.send(out.at[z], out.at[z], "z", step) for step in (1, 2, 3)]
    yield
    for copy in copies:
        copy.wait_recv()


def small_column(links, own, out):
    core, y = links.here["core"], links.here["y"]
    out[core, y] = own[...]
    copies = [links.send(own, out.at[core, y], "y", step) for step in (1, 2, 3)]
    yield
    for copy in copies:
        copy.wait_recv()
    copy = links.send(out.at[core], out.at[core], "core")
    yield
    copy.wait_recv()


def call(kernel, name, number, copies, outs, out_specs, in_specs, scratch, vmem, operands):
    return pl.pallas_call(
        kernel,
        name=name,
        out_shape=outs,
        in_specs=in_specs,
        out_specs=out_specs,
        scratch_shapes=[pltpu.SemaphoreType.DMA((copies,)), pltpu.SemaphoreType.DMA((copies,))]
        + scratch,
        compiler_params=pltpu.CompilerParams(
            collective_id=number, has_side_effects=True, vmem_limit_bytes=vmem * 2**20
        ),
    )(*operands)


def shaped(shape, kind=LOW):
    return jax.ShapeDtypeStruct(shape, kind)


def front_kernel(
    own_a, unit_own, gains, seq, full_a, unit_all, gains_all, seq_all, send_sems, recv_sems, kept
):
    links = Links(send_sems, recv_sems)
    links.meet(PLANE + COLUMN)
    together(
        [
            small_plane(links, gains, gains_all),
            small_column(links, seq, seq_all),
            plane_gather(links, own_a, full_a, kept.at[0]),
            column_gather(links, unit_own, unit_all),
        ]
    )
    own = pltpu.make_async_copy(
        unit_own, unit_all.at[block_of(links.here["y"], links.here["core"])], kept.at[1]
    )
    own.start()
    own.wait()
    links.drain()


def turn_kernel(
    partial,
    x_own,
    own_b,
    own_c,
    dy_own,
    two_all,
    middle,
    full_b,
    full_c,
    dy_all,
    send_sems,
    recv_sems,
    kept,
    passed,
    near,
    far,
):
    links = Links(send_sems, recv_sems)
    links.meet(PLANE + COLUMN)
    spot = block_of(links.here["y"], links.here["core"])
    own_dy = pltpu.make_async_copy(dy_own, dy_all.at[spot], kept.at[2])
    own_dy.start()

    def done(window, total):
        value = full(x_own[window]) + total
        middle[window] = value
        two_all[spot, window] = low(scaled_rows(value)[0])

    def turn():
        yield from column_scatter(links, partial, passed, near, far, done)
        yield from column_gather(links, two_all.at[spot], two_all)
        yield from column_gather(links, dy_own, dy_all)

    def weights():
        yield from plane_gather(links, own_b, full_b, kept.at[0])
        yield from plane_gather(links, own_c, full_c, kept.at[1])

    together([turn(), weights()])
    own_dy.wait()
    links.drain()


def back_kernel(
    partial,
    down_part,
    grad_gu,
    grad_d,
    middle,
    dy_own,
    mid_all,
    grad_mid,
    result,
    sum_gu,
    sum_d,
    send_sems,
    recv_sems,
    passed,
    near,
    far,
    passed_two,
    near_two,
    far_two,
    *scratch,
):
    links = Links(send_sems, recv_sems)
    links.meet(PLANE + COLUMN)
    spot = block_of(links.here["y"], links.here["core"])

    def done(window, total):
        unit, inverse = scaled_rows(middle[window])
        value = full(dy_own[window]) + norm_back(total, unit, inverse)
        grad_mid[window] = value
        mid_all[spot, window] = low(value)

    def done_two(window, total):
        result[window] = low(middle[window] + total)

    def turn():
        yield from column_scatter(links, partial, passed, near, far, done)
        yield from column_gather(links, mid_all.at[spot], mid_all)
        yield from column_scatter(links, down_part, passed_two, near_two, far_two, done_two)

    together(
        [
            turn(),
            plane_scatter(links, grad_gu, sum_gu, *scratch[:5]),
            plane_scatter(links, grad_d, sum_d, *scratch[5:]),
        ]
    )
    links.drain()


def end_kernel(
    partial,
    grad_qkv,
    grad_o,
    sum_gu,
    sum_d,
    w_qkv,
    w_gu,
    gain_one,
    gain_two,
    grad_mid,
    x_own,
    result,
    small,
    grad_x,
    out_rows,
    all_qkv,
    all_o,
    all_gu,
    all_d,
    sums,
    send_sems,
    recv_sems,
    gains_all,
    column_all,
    row,
    turned,
    sum_qkv,
    passed,
    near,
    far,
    *scratch,
):
    links = Links(send_sems, recv_sems)
    links.meet(PLANE + COLUMN)
    here = links.here
    y, core = here["y"], here["core"]
    half = lax.rem(y, 2)
    part = lax.div(y, 2) * 2 + core
    other = lax.rem(y + 2, 4)
    part_other = lax.div(other, 2) * 2 + core

    def share(out):
        across = links.send(out.at[part], out.at[part], "y", 2)
        beside = links.send(out.at[part], out.at[part], "core")
        yield
        across.wait_recv()
        second = links.send(out.at[part_other], out.at[part_other], "core")
        yield
        beside.wait_recv()
        second.wait_recv()

    def exchange(ref):
        copy = links.send(ref.at[half], ref.at[half], "pair")
        yield
        copy.wait_recv()

    def scale_gu(window):
        all_gu[part, window] = low(full(sum_gu[window]) * gain_two[window])
        part_sum = jnp.sum(full(sum_gu[window]) * full(w_gu[window]), 1, keepdims=True)
        turned[1, window] = jnp.broadcast_to(part_sum, (16, 128))

    def scale_qkv(window):
        all_qkv[part, window] = low(full(sum_qkv[window]) * gain_one[window])
        part_sum = jnp.sum(full(sum_qkv[window]) * full(w_qkv[window]), 1, keepdims=True)
        turned[0, window] = jnp.broadcast_to(part_sum, (16, 128))

    def done(window, total):
        unit, inverse = scaled_rows(full(x_own[window]))
        grad_x[half, window] = low(grad_mid[window] + norm_back(total, unit, inverse))

    def rows_job():
        yield from column_scatter(links, partial, passed, near, far, done)
        yield from exchange(grad_x)

    def early():
        out_rows[half] = result[...]
        all_d[part] = sum_d[...]
        each(128, 16, scale_gu)
        yield
        yield from exchange(out_rows)
        yield from share(all_gu)
        yield from share(all_d)

    def late():
        yield from plane_scatter(links, grad_qkv, sum_qkv, *scratch[:5])
        each(128, 16, scale_qkv)
        row[0:2] = jnp.sum(gains_all[:, :, 0:2], (0, 1))
        row[2:3] = turned[0].T[0:1]
        row[3:4] = turned[1].T[0:1]
        row[4:8] = jnp.zeros((4, 128), WIDE)
        yield from share(all_qkv)
        yield from small_column(links, row, column_all)

    def late_o():
        yield from plane_scatter(links, grad_o, all_o.at[part], *scratch[5:])
        yield from share(all_o)

    together([late(), late_o(), rows_job(), early(), small_plane(links, small, gains_all)])
    sums[...] = jnp.sum(column_all[...], (0, 1))
    links.drain()


def per_device(
    tokens,
    segments,
    attn_gain,
    q_weight,
    k_weight,
    v_weight,
    q_gain,
    k_gain,
    o_weight,
    mlp_gain,
    gate_weight,
    up_weight,
    down_weight,
    cotangent,
):
    part = lax.axis_index("ctx")
    parts = lax.axis_size("ctx")
    half = lax.axis_index("tp")
    halves = lax.axis_size("tp")
    rows_here, width = tokens.shape
    seq_len = rows_here * parts
    own_rows = rows_here // halves
    blocks = parts * halves
    score_scale = HD ** (-0.5)

    def quarter(weight, dim):
        size = weight.shape[dim] // parts
        return lax.dynamic_slice_in_dim(weight, part * size, size, dim)

    def own(array):
        return lax.dynamic_slice_in_dim(array, half * own_rows, own_rows, 0)

    attn_gain_f = full(attn_gain)[:, None]
    mlp_gain_f = full(mlp_gain)[:, None]
    wq, wk, wv = quarter(q_weight, 1), quarter(k_weight, 1), quarter(v_weight, 1)
    wg, wu = quarter(gate_weight, 1), quarter(up_weight, 1)
    wo_t = quarter(o_weight, 0).T
    wd_t = quarter(down_weight, 0).T
    w_qkv = jnp.concatenate([wq, wk, wv], 1)
    w_gu = jnp.concatenate([wg, wu], 1)
    nq, nkv, nff = wq.shape[1], wk.shape[1], wg.shape[1]
    rows_w = q_weight.shape[0]
    na, nb, nc = 2 * nq + 2 * nkv, 2 * nff, nff
    send_a = jnp.concatenate([low(full(w_qkv) * attn_gain_f), wo_t], 1)
    send_b = low(full(w_gu) * mlp_gain_f)
    x_own = own(tokens)
    dy_own = own(cotangent)
    unit_own = low(scaled_rows(full(x_own))[0])
    few = q_gain.shape[0]
    gains_own = jnp.zeros((8, 128), WIDE).at[0, :few].set(full(q_gain)).at[1, :few].set(full(k_gain))
    seq_own = jnp.broadcast_to(own(segments)[None, :], (8, 128))

    full_a, unit_all, gains_all, seq_all = call(
        front_kernel,
        "front",
        0,
        64,
        (
            shaped((4, 4, rows_w, na)),
            shaped((blocks, own_rows, width)),
            shaped((4, 4, 8, 128), WIDE),
            shaped((2, 4, 8, 128), jnp.int32),
        ),
        [HBM, HBM, VMEM, VMEM],
        [HBM, HBM, VMEM, VMEM],
        [pltpu.SemaphoreType.DMA((2,))],
        40,
        (send_a, unit_own, gains_own, seq_own),
    )
    full_a = full_a.reshape(16 * rows_w, na)
    unit_all = unit_all.reshape(seq_len, width)
    query_gain_f = gains_all[:, :, 0, :few].reshape(HD)
    key_gain_f = gains_all[:, :, 1, :few].reshape(HD)
    seq_ids = jnp.swapaxes(seq_all[:, :, 0].reshape(2, 2, 2, 128), 0, 1).reshape(seq_len)
    full_qkv = full_a[:, : nq + 2 * nkv]
    full_o_t = full_a[:, nq + 2 * nkv :]

    index = jnp.arange(seq_len, dtype=jnp.int32)
    count_0 = jnp.sum((seq_ids == 0).astype(jnp.int32))
    count_1 = jnp.sum((seq_ids == 1).astype(jnp.int32))
    position = index - jnp.where(
        seq_ids == 0, 0, jnp.where(seq_ids == 1, count_0, count_0 + count_1)
    )
    frequency = jnp.power(rope_base, -2.0 * jnp.arange(HD // 2, dtype=WIDE) / HD)
    angles = position.astype(WIDE)[:, None] * frequency[None, :]
    cosine = jnp.cos(angles)[:, None, :]
    sine = jnp.sin(angles)[:, None, :]
    allowed = (index[None, :] <= index[:, None]) & (seq_ids[None, :] == seq_ids[:, None])

    qkv = dot_nn(unit_all, full_qkv)
    query_proj = qkv[:, :nq].reshape(seq_len, nq // HD, HD)
    key_proj = qkv[:, nq : nq + nkv].reshape(seq_len, nkv // HD, HD)
    values = low(qkv[:, nq + nkv :]).reshape(seq_len, nkv // HD, HD)
    query_unit, query_inverse = scaled_rows(query_proj)
    key_unit, key_inverse = scaled_rows(key_proj)
    group = nq // nkv
    queries = low(rotate(query_unit * query_gain_f, cosine, sine, 1.0))
    keys = low(rotate(key_unit * key_gain_f, cosine, sine, 1.0))
    query_four = queries.reshape(seq_len, nkv // HD, group, HD)
    scores = (
        jnp.einsum("ignd,jgd->gnij", query_four, keys, preferred_element_type=WIDE) * score_scale
    )
    masked = jnp.where(allowed, scores, -jnp.inf)
    exponent = jnp.exp(masked - jnp.max(masked, -1, keepdims=True))
    probs = exponent / jnp.sum(exponent, -1, keepdims=True)
    attended = low(
        jnp.einsum("gnij,jgd->ignd", low(probs), values, preferred_element_type=WIDE)
    ).reshape(seq_len, nq)
    attn_part = low(dot_nt(attended, full_o_t)).reshape(blocks, own_rows, width)

    two_all, middle, full_b, full_c, dy_all = call(
        turn_kernel,
        "turn",
        1,
        96,
        (
            shaped((blocks, own_rows, width)),
            shaped((own_rows, width), WIDE),
            shaped((4, 4, rows_w, nb)),
            shaped((4, 4, rows_w, nc)),
            shaped((blocks, own_rows, width)),
        ),
        [VMEM, VMEM, HBM, HBM, HBM],
        [VMEM, VMEM, HBM, HBM, HBM],
        [pltpu.SemaphoreType.DMA((3,))] + column_scratch(),
        40,
        (attn_part, x_own, send_b, wd_t, dy_own),
    )
    two_all = two_all.reshape(seq_len, width)
    dy_all = dy_all.reshape(seq_len, width)
    full_b = full_b.reshape(16 * rows_w, nb)
    full_c = full_c.reshape(16 * rows_w, nc)

    gate_up = dot_nn(two_all, full_b)
    gate_act, up_act = gate_up[:, :nff], gate_up[:, nff:]
    sigmoid_gate = jax.nn.sigmoid(gate_act)
    silu_gate = gate_act * sigmoid_gate
    product = low(silu_gate * up_act)
    down_part = low(dot_nt(product, full_c)).reshape(blocks, own_rows, width)
    grad_product = dot_nn(dy_all, full_c)
    grad_d = low(dot_tn(dy_all, product))
    grad_gate = low(
        grad_product * up_act * sigmoid_gate * (1.0 + gate_act * (1.0 - sigmoid_gate))
    )
    grad_up = low(grad_product * silu_gate)
    grad_gu = jnp.concatenate([grad_gate, grad_up], 1)
    grad_two_part = low(dot_nt(grad_gu, full_b)).reshape(blocks, own_rows, width)
    grad_gu_w = low(dot_tn(two_all, grad_gu))

    mid_all, grad_mid, result, sum_gu, sum_d = call(
        back_kernel,
        "back",
        2,
        112,
        (
            shaped((blocks, own_rows, width)),
            shaped((own_rows, width), WIDE),
            shaped((own_rows, width)),
            shaped((rows_w, nb)),
            shaped((rows_w, nc)),
        ),
        [VMEM] * 5,
        [VMEM] * 6,
        column_scratch() + column_scratch() + plane_scratch(nb) + plane_scratch(nc),
        60,
        (
            grad_two_part,
            down_part,
            grad_gu_w.reshape(4, 4, rows_w, nb),
            grad_d.reshape(4, 4, rows_w, nc),
            middle,
            dy_own,
        ),
    )
    mid_all = mid_all.reshape(seq_len, width)

    grad_o_t = low(dot_tn(mid_all, attended))
    grad_attended = low(dot_nn(mid_all, full_o_t))
    grad_four = grad_attended.reshape(seq_len, nkv // HD, group, HD)
    grad_probs = jnp.einsum("ignd,jgd->gnij", grad_four, values, preferred_element_type=WIDE)
    row_dot = jnp.sum(probs * grad_probs, -1, keepdims=True)
    grad_scores = low(probs * (grad_probs - row_dot))
    grad_queries = (
        jnp.einsum("gnij,jgd->ignd", grad_scores, keys, preferred_element_type=WIDE) * score_scale
    )
    grad_keys = (
        jnp.einsum("gnij,ignd->jgd", grad_scores, query_four, preferred_element_type=WIDE)
        * score_scale
    )
    grad_values = jnp.einsum("gnij,ignd->jgd", low(probs), grad_four, preferred_element_type=WIDE)
    query_back = rotate(grad_queries.reshape(seq_len, nq // HD, HD), cosine, sine, -1.0)
    grad_qg_part = jnp.sum(query_back * query_unit, (0, 1))
    grad_q_proj = low(norm_back(query_back * query_gain_f, query_unit, query_inverse))
    key_back = rotate(grad_keys, cosine, sine, -1.0)
    grad_kg_part = jnp.sum(key_back * key_unit, (0, 1))
    grad_k_proj = low(norm_back(key_back * key_gain_f, key_unit, key_inverse))
    grad_qkv = jnp.concatenate(
        [
            grad_q_proj.reshape(seq_len, nq),
            grad_k_proj.reshape(seq_len, nkv),
            low(grad_values).reshape(seq_len, nkv),
        ],
        1,
    )
    grad_one_part = low(dot_nt(grad_qkv, full_qkv)).reshape(blocks, own_rows, width)
    grad_qkv_w = low(dot_tn(unit_all, grad_qkv))
    small = jnp.zeros((8, 128), WIDE).at[0].set(grad_qg_part).at[1].set(grad_kg_part)

    grad_x, out_rows, all_qkv, all_o, all_gu, all_d, sums = call(
        end_kernel,
        "end",
        3,
        112,
        (
            shaped((halves, own_rows, width)),
            shaped((halves, own_rows, width)),
            shaped((parts, rows_w, nq + 2 * nkv)),
            shaped((parts, rows_w, nq)),
            shaped((parts, rows_w, nb)),
            shaped((parts, rows_w, nc)),
            shaped((8, 128), WIDE),
        ),
        [VMEM] * 7,
        [VMEM] * 13,
        [
            pltpu.VMEM((4, 4, 8, 128), WIDE),
            pltpu.VMEM((2, 4, 8, 128), WIDE),
            pltpu.VMEM((8, 128), WIDE),
            pltpu.VMEM((2, 128, 128), WIDE),
            pltpu.VMEM((rows_w, nq + 2 * nkv), LOW),
        ]
        + column_scratch()
        + plane_scratch(nq + 2 * nkv)
        + plane_scratch(nq),
        60,
        (
            grad_one_part,
            grad_qkv_w.reshape(4, 4, rows_w, nq + 2 * nkv),
            grad_o_t.reshape(4, 4, rows_w, nq),
            sum_gu,
            sum_d,
            w_qkv,
            w_gu,
            attn_gain_f,
            mlp_gain_f,
            grad_mid,
            x_own,
            result,
            small,
        ),
    )

    def columns(piece):
        return full(jnp.swapaxes(piece, 0, 1).reshape(rows_w, -1))

    def rows(piece):
        return full(jnp.swapaxes(piece, 1, 2).reshape(-1, rows_w))

    sum_qk = lax.dynamic_slice_in_dim(sums[:2], lax.axis_index("fsdp") * few, few, 1)
    return (
        out_rows.reshape(rows_here, width),
        full(grad_x).reshape(rows_here, width),
        sums[2],
        columns(all_qkv[:, :, :nq]),
        columns(all_qkv[:, :, nq : nq + nkv]),
        columns(all_qkv[:, :, nq + nkv :]),
        sum_qk[0],
        sum_qk[1],
        rows(all_o),
        sums[3],
        columns(all_gu[:, :, :nff]),
        columns(all_gu[:, :, nff:]),
        rows(all_d),
    )


def solution(mesh):
    weight = P("fsdp", "tp")
    turned = P("tp", "fsdp")
    acts = P(("fsdp", "ctx"), None)
    gain = P("fsdp")
    return jax.shard_map(
        per_device,
        mesh=mesh,
        in_specs=(
            acts,
            P(("fsdp", "ctx")),
            gain,
            weight,
            weight,
            weight,
            gain,
            gain,
            turned,
            gain,
            weight,
            weight,
            turned,
            acts,
        ),
        out_specs=(
            acts,
            acts,
            gain,
            weight,
            weight,
            weight,
            gain,
            gain,
            turned,
            gain,
            weight,
            weight,
            turned,
        ),
        check_vma=False,
    )
```

time: 1190 us -> 473 us (0.40)
  waiting for transfers between devices: 853 us -> 0 us
  Pallas kernels: 0 us -> 296 us
  blocking collectives: 116 us -> 0 us
  other arithmetic: 52.5 us -> 38.3 us
  between operations: 16.9 us -> 3.22 us
    reduce_scatter x8 -> x0, waiting for transfers between devices: 526 us -> none  [the longest x4 250 us: scatter(): return lax.psum_scatter(grad, 'fsdp', scatter_dimension=0, tiled=True)]
    all_gather x10 -> x0, waiting for transfers between devices: 325 us -> none  [the longest x1 71 us: per_device(): two_all = lax.all_gather(low(unit_two), COLUMN, axis=0, tiled=True)]
    pallas_call x0 -> x4, Pallas kernels: none -> 296 us  [call(): pl.pallas_call(kernel, name=name, out_shape=outs, in_specs=in_specs, out_...]
    psum x2 -> x0, blocking collectives: 86.3 us -> none  [the longest x1 73.3 us: per_device(): lax.psum(jnp.concatenate([grad_qg_part, grad_kg_part]), ('fsdp', 'ctx', '...]
    all_gather x2 -> x0, blocking collectives: 29.8 us -> none  [the longest x1 18.9 us: per_device(): lax.all_gather(jnp.stack([q_gain, k_gain]), 'fsdp', axis=1, tiled=True)]
  transfers between devices with their start and end apart: 18 -> 0, of which waited for: 15 -> 0; matrix products, arithmetic and copies ran while one was open for 11% -> 0% of each run, Pallas kernels for 0% -> 0%
where the time goes in v2:
time: 473 us; the launch traced here: 464 us
  Pallas kernels  296 us (63%)
  matrix products  95.3 us (20%)
  other arithmetic  38.3 us (8%)
  local copies, waits for them, and re-layouts  31.4 us (7%)
    pallas_call x4, Pallas kernels, call(): pl.pallas_call(kernel, name=name, out_shape=outs, in_specs=in_specs, out_...  296 us
    dot_general x4, matrix products, dot_nn(): return jnp.dot(left, right, preferred_element_type=WIDE)  25 us
    dot_general x4, matrix products, dot_tn(): lax.dot_general(left, right, (((0,), (0,)), ((), ())), preferred_element_...  23.2 us
    dot_general x4, matrix products, dot_nt(): lax.dot_general(left, right, (((1,), (1,)), ((), ())), preferred_element_...  22.5 us
    unnamed x104, local copies, waits for them, and re-layouts  11.1 us

profile of v2, /device:TPU:1, one launch (start us, length us, event | category | flops | bytes accessed | tf_op | source)
XLA Modules:
  0.0 463.8 jit_solution(8708527405398386061)
XLA Ops:
  2.4 1.2 convert_bitcast_fusion.8
  4.7 1.2 fusion.32
  8.3 34.4 %front.1 = (bf16[4,4,128,768]{3,2,1,0:T(8,128)(2,1)S(1)}, bf16[8,128,2048]{2,1,0:T(8,128)(2,1)S(1)}, f32[4,4,8,128]{3,2,1,0:T(8,128)S(1)}, s32[2,4,8,128]{3,2,1,0:T(8,128)S(1)}) custom-call(bf16[128,768]{1,0:T(8,128)(2,1)S(1)} %pad_maximum_fusion.10.own_a, bf16[128,2048]{1,0:T(8,128)(2,1)S(1)} %fusion.33.unit_own, f32[8,128]{1,0:T(8,128)S(1)} %scatter.24.gains, ...), custom_call_target="tpu_custom_call" | custom-call | tf_op jit(solution)/shard_map/front/pallas_call | solution.py:433
  42.8 3.7 fusion.15
  46.5 1.1 multiply_reduce_fusion.4
  47.8 1.1 multiply_bitcast_fusion
  51.6 1.2 fusion.58
  52.7 3.1 broadcast_multiply_fusion
  55.8 2.5 slice.178
  58.3 1.5 copy.79
  59.9 1.7 multiply_reduce_fusion.1
  62.0 1.5 subtract_convert_fusion
  64.2 2.1 fusion.5
  66.3 2.0 fusion.4
  68.3 4.9 %fusion.18 = bf16[128,2,1024]{2,0,1:T(8,128)(2,1)S(1)} fusion(f32[1024,512]{0,1:T(8,128)} %fusion.15, f32[2,1024]{1,0:T(2,128)S(1)} %fusion.4, f32[2,1024]{1,0:T(2,128)S(1)} %get-tuple-element.167, f32[1024,1024,2]{1,0,2:T(8,128)S(1)} %get-tuple-element.168, pred[1024,1024]{0,1:T(8,128)(4,1)S(1)} %fusion.11), kind=kOutput, calls=%fused_computation.44 | convolution fusion | flops 547618816 | bytes 10240000 | tf_op jit(solution)/shard_map/gnij,jgd->ignd/dot_general | solution.py:775
  73.3 4.7 %convolution_convert_fusion.3 = bf16[1024,2048]{1,0:T(8,128)(2,1)} fusion(bf16[1024,256]{0,1:T(8,128)(2,1)S(1)} %bitcast.247, bf16[2048,768]{1,0:T(8,128)(2,1)} %bitcast.224), kind=kOutput, calls=%fused_computation.20 | convolution fusion | flops 1075838976 | bytes 5767168 | tf_op jit(solution)/shard_map/dot_general | solution.py:53
  81.0 77.9 %turn.1 = (bf16[8,128,2048]{2,1,0:T(8,128)(2,1)S(1)}, f32[128,2048]{1,0:T(8,128)S(1)}, bf16[4,4,128,1536]{3,2,1,0:T(8,128)(2,1)}, bf16[4,4,128,768]{3,2,1,0:T(8,128)(2,1)S(1)}, bf16[8,128,2048]{2,1,0:T(8,128)(2,1)S(1)}) custom-call(bf16[8,128,2048]{2,1,0:T(8,128)(2,1)} %bitcast.237, bf16[128,2048]{1,0:T(8,128)(2,1)S(1)} %get-tuple-element.138.x_own, ...), custom_call_target="tpu_custom_call" | custom-call | tf_op jit(solution)/shard_map/turn/pallas_call | solution.py:433
  158.9 10.9 %fusion.73 = f32[1024,1536]{0,1:T(8,128)} fusion(bf16[1024,2048]{1,0:T(8,128)(2,1)S(1)} %bitcast.229, bf16[2048,1536]{1,0:T(8,128)(2,1)} %bitcast.263), kind=kOutput, calls=%fused_computation.157 | convolution fusion | flops 6442450944 | bytes 16777216 | tf_op jit(solution)/shard_map/dot_general | solution.py:45
  169.8 6.8 %multiply_convert_fusion.2 = (bf16[1024,768]{0,1:T(8,128)(2,1)S(1)}, bf16[1024,768]{0,1:T(8,128)(2,1)S(1)}, bf16[1024,768]{0,1:T(8,128)(2,1)S(1)}) fusion(f32[1024,1536]{0,1:T(8,128)} %fusion.73, bf16[1024,2048]{1,0:T(8,128)(2,1)S(1)} %bitcast.231, bf16[2048,768]{1,0:T(8,128)(2,1)S(1)} %bitcast.233), kind=kOutput, calls=%fused_computation.26 | convolution fusion | flops 3233021952 | bytes 18350080 | tf_op jit(solution)/shard_map/dot_general | solution.py:45
  176.7 4.9 %convolution_convert_fusion.5 = bf16[2048,768]{1,0:T(8,128)(2,1)} fusion(bf16[1024,2048]{1,0:T(8,128)(2,1)S(1)} %bitcast.232, bf16[1024,768]{0,1:T(8,128)(2,1)S(1)} %get-tuple-element.141), kind=kOutput, calls=%fused_computation.22 | convolution fusion | flops 3222798336 | bytes 8912896 | tf_op jit(solution)/shard_map/dot_general | solution.py:49
  181.6 9.7 %convolution_convert_fusion = bf16[2048,1536]{1,0:T(8,128)(2,1)} fusion(bf16[1024,2048]{1,0:T(8,128)(2,1)S(1)} %bitcast.230, bf16[1024,768]{0,1:T(8,128)(2,1)S(1)} %get-tuple-element.140, bf16[1024,768]{0,1:T(8,128)(2,1)S(1)} %get-tuple-element.139), kind=kOutput, calls=%fused_computation.7 | convolution fusion | flops 6451888128 | bytes 13631488 | tf_op jit(solution)/shard_map/dot_general | solution.py:49
  191.3 5.1 %convolution_convert_fusion.4 = bf16[1024,2048]{1,0:T(8,128)(2,1)} fusion(bf16[1024,768]{0,1:T(8,128)(2,1)S(1)} %get-tuple-element.141, bf16[2048,768]{1,0:T(8,128)(2,1)S(1)} %bitcast.234), kind=kOutput, calls=%fused_computation.21 | convolution fusion | flops 3223322624 | bytes 8912896 | tf_op jit(solution)/shard_map/dot_general | solution.py:53
  196.4 8.3 %convolution_convert_fusion.1 = bf16[1024,2048]{1,0:T(8,128)(2,1)} fusion(bf16[2048,1536]{1,0:T(8,128)(2,1)S(1)} %bitcast.266, bf16[1024,768]{0,1:T(8,128)(2,1)S(1)} %get-tuple-element.140, bf16[1024,768]{0,1:T(8,128)(2,1)S(1)} %get-tuple-element.139), kind=kOutput, calls=%fused_computation.18 | convolution fusion | flops 6450839552 | bytes 13631488 | tf_op jit(solution)/shard_map/dot_general | solution.py:53
  204.7 96.8 %back.1 = (bf16[8,128,2048]{2,1,0:T(8,128)(2,1)}, f32[128,2048]{1,0:T(8,128)}, bf16[128,2048]{1,0:T(8,128)(2,1)}, bf16[128,1536]{1,0:T(8,128)(2,1)}, bf16[128,768]{1,0:T(8,128)(2,1)}) custom-call(bf16[8,128,2048]{2,1,0:T(8,128)(2,1)} %bitcast.243, bf16[8,128,2048]{2,1,0:T(8,128)(2,1)} %bitcast.242, bf16[4,4,128,1536]{3,2,1,0:T(8,128)(2,1)} %bitcast.240, ...), custom_call_target="tpu_custom_call" | custom-call | tf_op jit(solution)/shard_map/back/pallas_call | solution.py:433
  301.5 3.6 convolution_convert_fusion.8
  305.1 5.7 %fusion = (f32[2,1024]{1,0:T(2,128)S(1)}, f32[1024,1024,2]{1,0,2:T(8,128)S(1)}) fusion(f32[2,1024]{1,0:T(2,128)S(1)} %fusion.4, f32[2,1024]{1,0:T(2,128)S(1)} %get-tuple-element.167, f32[1024,1024,2]{1,0,2:T(8,128)} %copy-done.10, pred[1024,1024]{0,1:T(8,128)(4,1)S(1)} %copy-done.12, bf16[1024,2,128]{0,2,1:T(8,128)(2,1)S(1)} %bitcast.269, ...), kind=kOutput, calls=%fused_computation.3 | convolution fusion | flops 549451776 | bytes 18636800 | tf_op jit(solution)/shard_map/ignd,jgd->gnij/dot_general | solution.py:848
  311.3 2.8 fusion.6
  314.1 2.0 copy-done.9
  316.1 1.8 fusion.17
  318.5 1.6 multiply_reduce_fusion
  320.1 2.5 copy.89
  322.6 2.6 fusion.36
  325.3 4.4 fusion.25
  329.7 1.2 fusion.52
  331.5 1.2 multiply_reduce_fusion.2
  332.8 4.7 %convolution_convert_fusion.7 = bf16[2048,256]{1,0:T(8,128)(2,1)} fusion(bf16[1024,2048]{1,0:T(8,128)(2,1)} %bitcast.268, bf16[1024,256]{0,1:T(8,128)(2,1)} %bitcast.248), kind=kOutput, calls=%fused_computation.30 | convolution fusion | flops 1074266112 | bytes 5767168 | tf_op jit(solution)/shard_map/dot_general | solution.py:49
  337.6 1.2 multiply_convert_fusion.4
  338.8 5.6 %fusion.29 = bf16[1024,128]{0,1:T(8,128)(2,1)S(1)} fusion(bf16[1024,2,128]{0,2,1:T(8,128)(2,1)S(1)} %bitcast.270, f32[2,1024]{1,0:T(2,128)S(1)} %fusion.4, f32[2,1024]{1,0:T(2,128)S(1)} %get-tuple-element.167, f32[1024,1024,2]{1,0,2:T(8,128)} %copy-done.10, pred[1024,1024]{0,1:T(8,128)(4,1)S(1)} %copy-done.13), kind=kOutput, calls=%fused_computation.51 | convolution fusion | flops 547487744 | bytes 10240000 | tf_op jit(solution)/shard_map/gnij,ignd->jgd/dot_general | solution.py:858
  344.4 3.8 convolution_convert_fusion.6
  348.3 4.4 convolution_convert_fusion.2
  355.6 86.5 %end.1 = (bf16[2,128,2048]{2,1,0:T(8,128)(2,1)}, bf16[2,128,2048]{2,1,0:T(8,128)(2,1)}, bf16[4,128,512]{2,1,0:T(8,128)(2,1)}, bf16[4,128,256]{2,1,0:T(8,128)(2,1...) custom-call(bf16[8,128,2048]{2,1,0:T(8,128)(2,1)} %bitcast.241, ...), custom_call_target="tpu_custom_call" | custom-call | tf_op jit(solution)/shard_map/end/pallas_call | solution.py:433
  442.1 2.8 convert_bitcast_fusion.1
  444.9 1.9 copy.99
  446.8 1.6 copy.105
  448.9 1.6 copy.106
  450.5 1.3 convert_bitcast_fusion
  451.8 1.6 copy.101
  453.4 1.6 bitcast_convert_fusion
  (155 shorter events, 24.2 us)
Async XLA Ops:
  0.6 80.2 %copy-start = (bf16[256,2048]{1,0:T(8,128)(2,1)S(1)}, bf16[256,2048]{1,0:T(8,128)(2,1)}, u32[]{:S(2)}) copy-start(bf16[256,2048]{1,0:T(8,128)(2,1)} %param.35) | copy-start | bytes 3145732
  1.5 3.1 copy-start.33
  1.5 3.2 copy-start.35
  2.4 1.2 copy-start.30
  5.9 75.0 %copy-start.2 = (bf16[128,2048]{1,0:T(8,128)(2,1)}, bf16[128,2048]{1,0:T(8,128)(2,1)S(1)}, u32[]{:S(2)}) copy-start(bf16[128,2048]{1,0:T(8,128)(2,1)S(1)} %get-tuple-element.138.x_own) | copy-start | bytes 1572868
  42.7 3.8 copy-start.5
  42.8 3.8 copy-start.7
  55.8 7.7 %copy-start.16 = (f32[1024,64]{1,0:T(8,128)}, f32[1024,64]{1,0:T(8,128)S(1)}, u32[]{:S(2)}) copy-start(f32[1024,64]{1,0:T(8,128)S(1)} %get-tuple-element.158) | copy-start | bytes 786436
  59.8 4.3 copy-start.14
  63.5 2.8 copy-start.21
  63.6 2.8 copy-start.22
  64.2 4.1 copy-start.11
  66.3 6.9 %copy-start.10 = (f32[1024,1024,2]{1,0,2:T(8,128)}, f32[1024,1024,2]{1,0,2:T(8,128)S(1)}, u32[]{:S(2)}) copy-start(f32[1024,1024,2]{1,0,2:T(8,128)S(1)} %get-tuple-element.168) | copy-start | bytes 25165828
  73.2 4.8 %copy-start.27 = (bf16[128,2,1024]{2,0,1:T(8,128)(2,1)}, bf16[128,2,1024]{2,0,1:T(8,128)(2,1)S(1)}, u32[]{:S(2)}) copy-start(bf16[128,2,1024]{2,0,1:T(8,128)(2,1)S(1)} %fusion.18) | copy-start | bytes 1572868
  73.3 5.8 %copy-start.41 = (bf16[128]{0:T(256)(128)(2,1)S(1)}, bf16[128]{0:T(256)(128)(2,1)}, u32[]{:S(2)}) copy-start(bf16[128]{0:T(256)(128)(2,1)} %param.31) | copy-start | bytes 772
  79.1 0.7 copy-start.23
  79.1 0.7 copy-start.25
  81.0 88.9 %copy-start.3 = (bf16[128,2048]{1,0:T(8,128)(2,1)}, bf16[128,2048]{1,0:T(8,128)(2,1)S(1)}, u32[]{:S(2)}) copy-start(bf16[128,2048]{1,0:T(8,128)(2,1)S(1)} %constant_dynamic-slice_fusion.1.dy_own) | copy-start | bytes 1572868
  158.9 10.9 %copy-start.4 = (f32[128,2048]{1,0:T(8,128)}, f32[128,2048]{1,0:T(8,128)S(1)}, u32[]{:S(2)}) copy-start(f32[128,2048]{1,0:T(8,128)S(1)} %get-tuple-element.90.middle) | copy-start | bytes 3145732
  176.7 19.7 %slice-start.2 = ((s8[6291456]{0:T(1024)(128)(4,1)}), s8[4194304]{0:T(1024)(128)(4,1)S(1)}, s32[]{:S(2)}) async-start(s8[6291456]{0:T(1024)(128)(4,1)} %bitcast.264), calls=%async_computation.2 | async-start | bytes 8388608
  181.6 14.8 %slice-start.3 = ((s8[6291456]{0:T(1024)(128)(4,1)}), s8[2097152]{0:T(1024)(128)(4,1)S(1)}, s32[]{:S(2)}) async-start(s8[6291456]{0:T(1024)(128)(4,1)} %bitcast.264), calls=%async_computation.3 | async-start | bytes 4194304
  204.7 96.8 %copy-start.6 = (bf16[4,4,128,768]{3,2,1,0:T(8,128)(2,1)S(1)}, bf16[4,4,128,768]{3,2,1,0:T(8,128)(2,1)}, u32[]{:S(2)}) copy-start(bf16[4,4,128,768]{3,2,1,0:T(8,128)(2,1)} %copy-done.5) | copy-start | bytes 9437188
  301.5 3.6 copy-start.12
  305.1 5.8 %copy-start.42 = (bf16[1024,256]{0,1:T(8,128)(2,1)}, bf16[1024,256]{0,1:T(8,128)(2,1)S(1)}, u32[]{:S(2)}) copy-start(bf16[1024,256]{0,1:T(8,128)(2,1)S(1)} %convolution_convert_fusion.8) | copy-start | bytes 1572868
  305.1 5.8 %slice-start = ((s8[8388608]{0:T(1024)(128)(4,1)}), s8[4194304]{0:T(1024)(128)(4,1)S(1)}, s32[]{:S(2)}) async-start(s8[8388608]{0:T(1024)(128)(4,1)} %bitcast.235), calls=%async_computation | async-start | bytes 8388608
  305.1 6.2 %slice-start.1 = ((s8[8388608]{0:T(1024)(128)(4,1)}), s8[4194304]{0:T(1024)(128)(4,1)S(1)}, s32[]{:S(2)}) async-start(s8[8388608]{0:T(1024)(128)(4,1)} %bitcast.235), calls=%async_computation.1 | async-start | bytes 8388608
  314.1 2.0 copy-start.9
  316.1 1.9 copy-start.17
  316.1 1.9 copy-start.20
  316.1 2.4 copy-start.15
  330.8 0.7 copy-start.18
  332.8 6.0 %copy-start.38 = (f32[8,128]{1,0:T(8,128)}, f32[8,128]{1,0:T(8,128)S(1)}, u32[]{:S(2)}) copy-start(f32[8,128]{1,0:T(8,128)S(1)} %scatter.26.small) | copy-start | bytes 12292
  332.8 4.8 %copy-start.19 = (f32[1024,64]{0,1:T(8,128)S(1)}, f32[1024,64]{0,1:T(8,128)}, u32[]{:S(2)}) copy-start(f32[1024,64]{0,1:T(8,128)} %copy-done.18) | copy-start | bytes 786436
  332.8 6.0 %copy-start.13 = (pred[1024,1024]{0,1:T(8,128)(4,1)S(1)}, pred[1024,1024]{0,1:T(8,128)(4,1)}, u32[]{:S(2)}) copy-start(pred[1024,1024]{0,1:T(8,128)(4,1)} %copy-done.11) | copy-start | bytes 3145732
  332.8 6.0 %copy-start.43 = (bf16[1024,256]{0,1:T(8,128)(2,1)S(1)}, bf16[1024,256]{0,1:T(8,128)(2,1)}, u32[]{:S(2)}) copy-start(bf16[1024,256]{0,1:T(8,128)(2,1)} %copy-done.42) | copy-start | bytes 1572868
  338.8 5.6 %copy-start.8 = (bf16[8,128,2048]{2,1,0:T(8,128)(2,1)S(1)}, bf16[8,128,2048]{2,1,0:T(8,128)(2,1)}, u32[]{:S(2)}) copy-start(bf16[8,128,2048]{2,1,0:T(8,128)(2,1)} %copy-done.7) | copy-start | bytes 12582916
  338.8 5.6 %copy-start.32 = (bf16[1024,256]{0,1:T(8,128)(2,1)S(1)}, bf16[1024,256]{0,1:T(8,128)(2,1)}, u32[]{:S(2)}) copy-start(bf16[1024,256]{0,1:T(8,128)(2,1)} %get-tuple-element.143) | copy-start | bytes 1572868
  348.2 4.4 copy-start.31
  348.2 4.4 copy-start.34
  348.3 4.4 copy-start.36
  348.3 5.1 %copy-start.24 = (bf16[128,768]{1,0:T(8,128)(2,1)S(1)}, bf16[128,768]{1,0:T(8,128)(2,1)}, u32[]{:S(2)}) copy-start(bf16[128,768]{1,0:T(8,128)(2,1)} %copy-done.23) | copy-start | bytes 589828
  348.3 5.1 %copy-start.26 = (bf16[128,768]{1,0:T(8,128)(2,1)S(1)}, bf16[128,768]{1,0:T(8,128)(2,1)}, u32[]{:S(2)}) copy-start(bf16[128,768]{1,0:T(8,128)(2,1)} %copy-done.25) | copy-start | bytes 589828
  348.3 5.8 %copy-start.40 = (f32[128,1]{0,1:T(1,128)S(1)}, f32[128,1]{0,1:T(1,128)}, u32[]{:S(2)}) copy-start(f32[128,1]{0,1:T(1,128)} %get-tuple-element.165) | copy-start | bytes 1540
  448.9 4.5 copy-start.28
  453.4 6.9 %copy-start.37 = (bf16[4,128,256]{2,1,0:T(8,128)(2,1)S(1)}, bf16[4,128,256]{2,1,0:T(8,128)(2,1)}, u32[]{:S(2)}) copy-start(bf16[4,128,256]{2,1,0:T(8,128)(2,1)} %get-tuple-element.100) | copy-start | bytes 786436
  455.0 6.3 %copy-start.39 = (f32[8,128]{1,0:T(8,128)S(1)}, f32[8,128]{1,0:T(8,128)}, u32[]{:S(2)}) copy-start(f32[8,128]{1,0:T(8,128)} %get-tuple-element.98) | copy-start | bytes 12292
  455.0 7.4 %copy-start.29 = (bf16[2,128,2048]{2,1,0:T(8,128)(2,1)S(1)}, bf16[2,128,2048]{2,1,0:T(8,128)(2,1)}, u32[]{:S(2)}) copy-start(bf16[2,128,2048]{2,1,0:T(8,128)(2,1)} %get-tuple-element.96) | copy-start | bytes 3145732
  456.1 7.3 %copy-start.1 = (bf16[256,2048]{1,0:T(8,128)(2,1)S(1)}, bf16[256,2048]{1,0:T(8,128)(2,1)}, u32[]{:S(2)}) copy-start(bf16[256,2048]{1,0:T(8,128)(2,1)} %param.35) | copy-start | bytes 3145732
